TPU v7x, 512 devices: a whole 4x4x16 slice. The times are simulated.
512 devices in a mesh: tile: 64 (over x_hi, z, core), sec: 8 (over x_lo, y).
Axes of the slice: x: 4 (x_hi: 2, x_lo: 2; x = x_hi * 2 + x_lo), y: 4, z: 16, core: 2. Of those that a mesh axis runs over, the one named last changes fastest.
Arguments:
- obj: float32 [2, 8, 8192, 256], P(None, 'sec', 'tile'), may hold values from -1.25 to 1.25, as said below
- probe: float32 [2, 4, 128, 128], replicated, may hold values from -3 to 3
- measured: float32 [128, 128, 128], P('tile'), may hold values from 0.5 to 4
- row_offset: int32 [128], P('tile'), may hold values from 0 to 127
- col_offset: int32 [128], P('tile'), may hold values from 0 to 128
Outputs:
- obj_grad: float32 [2, 8, 8192, 256], P(None, 'sec', 'tile')
- probe_grad: float32 [2, 4, 128, 128], P(None, None, 'sec')
Inputs may be any that keep to these rules, and one draw needn't show every extreme that they name: `obj`: real and imaginary parts of a transmission of magnitude 0.75 to 1.25.
All inputs are finite; a program needn't handle non-finite values.
Results may differ from a plain program's by a relative error of at most 0.0003.
Values sent between devices are 32-bit elements; how exact they have to be, the bound alone decides.
No kernel may reach another device: no remote copies, remote signals or barrier semaphores. Data moves between devices by JAX's collectives and lax.ppermute only.
A program may use at most 64 MiB of HBM per device.

v0:
```python
import math

import jax
import jax.numpy as jnp
from jax import lax
from jax.sharding import PartitionSpec as P

PHASE_RATE = 0.05
HIGH = lax.Precision.HIGHEST


def shifted(shard, axis, by):
    count = lax.axis_size(axis)
    return lax.ppermute(shard, axis, [(i, (i + by) % count) for i in range(count)])


def passed_along(block, axis, distance):
    devices = range(lax.axis_size(axis))
    route = [(i - distance, i) for i in devices if i - distance in devices]
    return lax.ppermute(block, axis, route)


def from_root(value, axis, source):
    kept = jnp.where(lax.axis_index(axis) == source, value, 0).astype(value.dtype)
    return lax.psum(kept, axis)


def optics(size):
    index = jnp.arange(size, dtype=jnp.int32)
    product = index[:, None] * index[None, :] % size
    angle = product.astype(jnp.float32) * (2.0 * math.pi / size)
    norm_scale = 1.0 / math.sqrt(size)
    four_re = jnp.cos(angle) * norm_scale
    four_im = -jnp.sin(angle) * norm_scale
    freq = (index + size // 2) % size - size // 2
    phase = (freq * freq).astype(jnp.float32) * PHASE_RATE
    kern_re = jnp.cos(phase)
    kern_im = -jnp.sin(phase)
    scaled_re = kern_re[:, None] * four_re - kern_im[:, None] * four_im
    scaled_im = kern_re[:, None] * four_im + kern_im[:, None] * four_re
    prop_re = jnp.dot(four_re, scaled_re, precision=HIGH) + jnp.dot(
        four_im, scaled_im, precision=HIGH
    )
    prop_im = jnp.dot(four_re, scaled_im, precision=HIGH) - jnp.dot(
        four_im, scaled_re, precision=HIGH
    )
    return (four_re, four_im, prop_re, prop_im)


def left_mult(matrix, field):
    return jnp.einsum("ab,...bc->...ac", matrix, field, precision=HIGH)


def right_mult(field, matrix):
    return jnp.einsum("...ac,dc->...ad", field, matrix, precision=HIGH)


def sandwich(mat_re, mat_im, field_re, field_im):
    half_re = left_mult(mat_re, field_re) - left_mult(mat_im, field_im)
    half_im = left_mult(mat_re, field_im) + left_mult(mat_im, field_re)
    out_re = right_mult(half_re, mat_re) - right_mult(half_im, mat_im)
    out_im = right_mult(half_re, mat_im) + right_mult(half_im, mat_re)
    return (out_re, out_im)


def per_device(obj, probe, measured, row_offset, col_offset):
    size = probe.shape[-1]
    modes = probe.shape[1]
    own_rows = obj.shape[2]
    own_cols = obj.shape[3]
    count = measured.shape[0]
    four_re, four_im, prop_re, prop_im = optics(size)
    segment = lax.axis_index("sec")
    segments = lax.axis_size("sec")
    rim_rows = shifted(obj, "tile", -1)
    extended = jnp.concatenate([obj, rim_rows], axis=2)[:, 0]

    def cut_window(row_first, col_first):
        return lax.dynamic_slice(extended, (0, row_first, col_first), (2, size, size))

    windows = jax.vmap(cut_window)(row_offset, col_offset)
    blocks = 1
    block_size = count // blocks
    wave_shape = (block_size, 2, modes, size, size)
    probe_block = jnp.broadcast_to(probe, wave_shape)
    total_steps = blocks + segments - 1

    def forward_work(step, stored, final, incoming):
        micro = step - segment
        is_live = jnp.logical_and(micro >= 0, micro < blocks)

        def work(operands):
            stored_in, final_in, arriving = operands
            wave_in = jnp.where(segment == 0, probe_block, arriving)
            obj_re = windows[:, 0, None]
            obj_im = windows[:, 1, None]
            exit_re = wave_in[:, 0] * obj_re - wave_in[:, 1] * obj_im
            exit_im = wave_in[:, 0] * obj_im + wave_in[:, 1] * obj_re
            next_re, next_im = sandwich(prop_re, prop_im, exit_re, exit_im)
            leaving = jnp.stack([next_re, next_im], axis=1)
            return (wave_in, leaving, leaving)

        def forward_skip_work(operands):
            stored_in, final_in, arriving = operands
            return (stored_in, final_in, jnp.zeros_like(arriving))

        return lax.cond(is_live, work, forward_skip_work, (stored, final, incoming))

    def forward_step(step, state_all):
        stored, final, incoming = state_all
        stored, final, leaving = forward_work(step, stored, final, incoming)
        incoming = passed_along(leaving, "sec", 1)
        return (stored, final, incoming)

    zero_waves = jnp.zeros((count, 2, modes, size, size), jnp.float32)
    stored, final, incoming = lax.fori_loop(
        0,
        total_steps - 1,
        forward_step,
        (zero_waves, zero_waves, jnp.zeros(wave_shape, jnp.float32)),
    )
    stored, final, _ = forward_work(total_steps - 1, stored, final, incoming)

    def far_gradient(final_waves):
        far_re, far_im = sandwich(four_re, four_im, final_waves[:, 0], final_waves[:, 1])
        intensity = jnp.sum(far_re * far_re + far_im * far_im, axis=1)
        weight_res = 2.0 * (intensity - measured)[:, None]
        back_re, back_im = sandwich(four_re.T, -four_im.T, weight_res * far_re, weight_res * far_im)
        return jnp.stack([back_re, back_im], axis=1)

    def no_gradient(final_waves):
        return jnp.zeros_like(final_waves)

    grad_last = lax.cond(segment == segments - 1, far_gradient, no_gradient, final)

    def backward_work(step, window_grads, probe_acc, incoming):
        micro = step - (segments - 1 - segment)
        is_live = jnp.logical_and(micro >= 0, micro < blocks)

        def work(operands):
            grads_in, acc_in, arriving = operands
            grad_out = jnp.where(segment == segments - 1, grad_last, arriving)
            grad_re, grad_im = sandwich(prop_re.T, -prop_im.T, grad_out[:, 0], grad_out[:, 1])
            obj_re = windows[:, 0, None]
            obj_im = windows[:, 1, None]
            win_re = jnp.sum(stored[:, 0] * grad_re + stored[:, 1] * grad_im, axis=1)
            win_im = jnp.sum(stored[:, 0] * grad_im - stored[:, 1] * grad_re, axis=1)
            grads_out = jnp.stack([win_re, win_im], axis=1)
            back_re = obj_re * grad_re + obj_im * grad_im
            back_im = obj_re * grad_im - obj_im * grad_re
            leaving = jnp.stack([back_re, back_im], axis=1)
            return (grads_out, acc_in + jnp.sum(leaving, axis=0), leaving)

        def backward_skip_work(operands):
            grads_in, acc_in, arriving = operands
            return (grads_in, acc_in, jnp.zeros_like(arriving))

        return lax.cond(is_live, work, backward_skip_work, (window_grads, probe_acc, incoming))

    def backward_step(step, state_all):
        window_grads, probe_acc, incoming = state_all
        window_grads, probe_acc, leaving = backward_work(step, window_grads, probe_acc, incoming)
        incoming = passed_along(leaving, "sec", -1)
        return (window_grads, probe_acc, incoming)

    start_state = (
        jnp.zeros((count, 2, size, size), jnp.float32),
        jnp.zeros_like(probe),
        jnp.zeros(wave_shape, jnp.float32),
    )
    window_grads, probe_acc, incoming = lax.fori_loop(
        0, total_steps - 1, backward_step, start_state
    )
    window_grads, probe_acc, _ = backward_work(total_steps - 1, window_grads, probe_acc, incoming)

    def scatter_window(position, grid):
        row_first = row_offset[position]
        col_first = col_offset[position]
        before = lax.dynamic_slice(grid, (0, row_first, col_first), (2, size, size))
        return lax.dynamic_update_slice(
            grid, before + window_grads[position], (0, row_first, col_first)
        )

    grid_grad = lax.fori_loop(
        0, count, scatter_window, jnp.zeros((2, own_rows + size, own_cols), jnp.float32)
    )
    arrived = shifted(grid_grad[:, own_rows:], "tile", 1)
    owned = grid_grad[:, :own_rows]
    owned = jnp.concatenate([owned + arrived, owned[:, size:]], axis=1)
    obj_grad = owned[:, None]
    own_probe = jnp.where(segment == 0, probe_acc, jnp.zeros_like(probe_acc))
    tile_total = lax.psum(own_probe, "tile")
    probe_total = from_root(tile_total, "sec", 0)
    band = size // segments
    my_rows = lax.dynamic_slice_in_dim(probe_total, segment * band, band, 2)
    probe_grad = my_rows / (count * lax.axis_size("tile"))
    return (obj_grad, probe_grad)


def solution(mesh):
    return jax.shard_map(
        per_device,
        mesh=mesh,
        in_specs=(P(None, "sec", "tile", None), P(), P("tile", None, None), P("tile"), P("tile")),
        out_specs=(P(None, "sec", "tile", None), P(None, None, "sec", None)),
        check_vma=False,
    )
```

profile of v0, /device:TPU:1, one launch (start us, length us, event | category | flops | bytes accessed | tf_op | source)
XLA Modules:
  0.0 1209.0 jit_solution(12963402729089470383)
XLA Ops:
  7.2 8.8 collective-permute-start.2
  19.9 4.1 while.52
  20.6 1.4 bitcast_dynamic-update-slice_fusion.2
  22.6 1.4 bitcast_dynamic-update-slice_fusion.2
  24.7 1.1 broadcast.114
  25.8 1.1 broadcast.114.clone2
  27.0 194.5 %while.53 = (s32[]{:T(128)}, f32[2,2,4,128,128]{3,4,2,0,1:T(8,128)}, f32[2,2,4,128,128]{4,3,2,0,1:T(8,128)}, f32[2,2,4,128,128]{4,3,2,0,1:T(8,128)S(1)}, s32[]{:...) while((s32[]{:T(128)}, ...), condition=%wide.region_3.4_spmd.clone, body=%wide.region_0.3_spmd.clone.sunk | while | flops 1613234176 | bytes 27787548 | solution.py:116
  27.0 15.0 %conditional.12 = (f32[2,2,4,128,128]{3,4,2,0,1:T(8,128)}, f32[2,2,4,128,128]{4,3,2,0,1:T(8,128)}, f32[2,2,4,128,128]{4,3,2,0,1:T(8,128)S(1)}) conditional(s32[]{:T(128)} %convert_element_type.132, (f32[2,2,4,128,128]{3,4,2,0,1:T(8,128)}, f32[2,2,4,128,128]{4,3,2,0,1:T(8,128)}) %tuple.179, (s32[]{:T(128)}, f32[2,4,128,128]{2,3,1,0:T(8,128)S(1)}, ...), branch_computations={%region_1.1_spmd, %region_2.2_spmd} | conditional | flops 1613234176 | bytes 23592994 | solution.py:107
  27.4 1.1 broadcast_select_fusion
  28.5 1.8 fusion.12
  30.3 1.8 fusion.4
  32.1 1.8 fusion.16
  33.9 1.8 fusion.5
  39.7 1.1 pad_maximum_fusion
  40.8 1.2 copy.130
  42.0 1.3 collective-permute-start.1
  43.4 16.3 %collective-permute-done.1 = f32[2,2,4,128,128]{4,3,2,0,1:T(8,128)S(1)} collective-permute-done((f32[2,2,4,128,128]{4,3,2,0,1:T(8,128)S(1)}, f32[2,2,4,128,128]{4,3,2,0,1:T(8,128)S(1)}, u32[]{:S(2)}, u32[]{:S(2)}) %collective-permute-start.1) | collective-permute-done | bytes 1048608 | tf_op jit(solution)/shard_map/while/body/eval_jaxpr/ppermute | solution.py:20
  59.8 19.0 %collective-permute-start.1 = (f32[2,2,4,128,128]{4,3,2,0,1:T(8,128)S(1)}, f32[2,2,4,128,128]{4,3,2,0,1:T(8,128)S(1)}, u32[]{:S(2)}, u32[]{:S(2)}) collective-permute-start(f32[2,2,4,128,128]{4,3,2,0,1:T(8,128)S(1)} %get-tuple-element.1046), channel_id=1, source_target_pairs={{0,1},{1,2},{2,3},{3,4},{4,5},{5,6},{6,7},{8,9},{9,10},{10,11},{11... | collective-permute-start | bytes 3145736 | tf_op jit(solution)/shard_map/while/body/eval_jaxpr/ppermute | solution.py:20
  78.8 15.4 %collective-permute-done.1 = f32[2,2,4,128,128]{4,3,2,0,1:T(8,128)S(1)} collective-permute-done((f32[2,2,4,128,128]{4,3,2,0,1:T(8,128)S(1)}, f32[2,2,4,128,128]{4,3,2,0,1:T(8,128)S(1)}, u32[]{:S(2)}, u32[]{:S(2)}) %collective-permute-start.1) | collective-permute-done | bytes 1048608 | tf_op jit(solution)/shard_map/while/body/eval_jaxpr/ppermute | solution.py:20
  94.3 4.2 collective-permute-start.1
  98.5 17.3 %collective-permute-done.1 = f32[2,2,4,128,128]{4,3,2,0,1:T(8,128)S(1)} collective-permute-done((f32[2,2,4,128,128]{4,3,2,0,1:T(8,128)S(1)}, f32[2,2,4,128,128]{4,3,2,0,1:T(8,128)S(1)}, u32[]{:S(2)}, u32[]{:S(2)}) %collective-permute-start.1) | collective-permute-done | bytes 1048608 | tf_op jit(solution)/shard_map/while/body/eval_jaxpr/ppermute | solution.py:20
  115.9 14.5 %collective-permute-start.1 = (f32[2,2,4,128,128]{4,3,2,0,1:T(8,128)S(1)}, f32[2,2,4,128,128]{4,3,2,0,1:T(8,128)S(1)}, u32[]{:S(2)}, u32[]{:S(2)}) collective-permute-start(f32[2,2,4,128,128]{4,3,2,0,1:T(8,128)S(1)} %get-tuple-element.1046), channel_id=1, source_target_pairs={{0,1},{1,2},{2,3},{3,4},{4,5},{5,6},{6,7},{8,9},{9,10},{10,11},{11... | collective-permute-start | bytes 3145736 | tf_op jit(solution)/shard_map/while/body/eval_jaxpr/ppermute | solution.py:20
  130.4 11.7 collective-permute-done.1
  142.2 9.8 collective-permute-start.1
  152.0 17.0 %collective-permute-done.1 = f32[2,2,4,128,128]{4,3,2,0,1:T(8,128)S(1)} collective-permute-done((f32[2,2,4,128,128]{4,3,2,0,1:T(8,128)S(1)}, f32[2,2,4,128,128]{4,3,2,0,1:T(8,128)S(1)}, u32[]{:S(2)}, u32[]{:S(2)}) %collective-permute-start.1) | collective-permute-done | bytes 1048608 | tf_op jit(solution)/shard_map/while/body/eval_jaxpr/ppermute | solution.py:20
  169.1 8.5 collective-permute-start.1
  177.6 11.7 collective-permute-done.1
  189.4 15.5 %collective-permute-start.1 = (f32[2,2,4,128,128]{4,3,2,0,1:T(8,128)S(1)}, f32[2,2,4,128,128]{4,3,2,0,1:T(8,128)S(1)}, u32[]{:S(2)}, u32[]{:S(2)}) collective-permute-start(f32[2,2,4,128,128]{4,3,2,0,1:T(8,128)S(1)} %get-tuple-element.1046), channel_id=1, source_target_pairs={{0,1},{1,2},{2,3},{3,4},{4,5},{5,6},{6,7},{8,9},{9,10},{10,11},{11... | collective-permute-start | bytes 3145736 | tf_op jit(solution)/shard_map/while/body/eval_jaxpr/ppermute | solution.py:20
  204.9 16.6 %collective-permute-done.1 = f32[2,2,4,128,128]{4,3,2,0,1:T(8,128)S(1)} collective-permute-done((f32[2,2,4,128,128]{4,3,2,0,1:T(8,128)S(1)}, f32[2,2,4,128,128]{4,3,2,0,1:T(8,128)S(1)}, u32[]{:S(2)}, u32[]{:S(2)}) %collective-permute-start.1) | collective-permute-done | bytes 1048608 | tf_op jit(solution)/shard_map/while/body/eval_jaxpr/ppermute | solution.py:20
  221.5 16.5 %conditional.5 = (f32[2,2,4,128,128]{3,4,2,0,1:T(8,128)}, f32[2,2,4,128,128]{4,3,2,0,1:T(8,128)}, f32[2,2,4,128,128]{4,3,2,0,1:T(8,128)S(1)}) conditional(s32[]{:T(128)} %convert_element_type.92, (f32[2,2,4,128,128]{3,4,2,0,1:T(8,128)}, f32[2,2,4,128,128]{4,3,2,0,1:T(8,128)}) %tuple.91, (s32[]{:T(128)}, f32[2,4,128,128]{2,3,1,0:T(8,128)S(1)}, ...), branch_computations={%region_4.5_spmd, %region_5.6_spmd} | conditional | flops 1613234176 | bytes 25165886 | solution.py:107
  221.5 1.6 copy.111
  242.0 238.4 %while.50 = (s32[]{:T(128)}, f32[2,2,128,128]{3,2,0,1:T(8,128)}, f32[2,4,128,128]{3,2,1,0:T(8,128)}, f32[2,2,4,128,128]{4,3,2,0,1:T(8,128)S(1)}, s32[]{:T(128)},...) while((s32[]{:T(128)}, f32[2,2,128,128]{3,2,0,1:T(8,128)}, ...), condition=%wide.region_15.16_spmd, body=%wide.region_9.15_spmd.sunk | while | flops 1613824000 | bytes 32506200 | solution.py:171
  242.1 1.3 collective-permute-start
  243.4 15.6 %collective-permute-done = f32[2,2,4,128,128]{4,3,2,0,1:T(8,128)S(1)} collective-permute-done((f32[2,2,4,128,128]{4,3,2,0,1:T(8,128)S(1)}, f32[2,2,4,128,128]{4,3,2,0,1:T(8,128)S(1)}, u32[]{:S(2)}, u32[]{:S(2)}) %collective-permute-start) | collective-permute-done | bytes 1048608 | tf_op jit(solution)/shard_map/while/body/eval_jaxpr/ppermute | solution.py:20
  259.1 1.3 collective-permute-start
  260.4 27.7 %collective-permute-done = f32[2,2,4,128,128]{4,3,2,0,1:T(8,128)S(1)} collective-permute-done((f32[2,2,4,128,128]{4,3,2,0,1:T(8,128)S(1)}, f32[2,2,4,128,128]{4,3,2,0,1:T(8,128)S(1)}, u32[]{:S(2)}, u32[]{:S(2)}) %collective-permute-start) | collective-permute-done | bytes 1048608 | tf_op jit(solution)/shard_map/while/body/eval_jaxpr/ppermute | solution.py:20
  288.3 1.3 collective-permute-start
  289.6 22.3 %collective-permute-done = f32[2,2,4,128,128]{4,3,2,0,1:T(8,128)S(1)} collective-permute-done((f32[2,2,4,128,128]{4,3,2,0,1:T(8,128)S(1)}, f32[2,2,4,128,128]{4,3,2,0,1:T(8,128)S(1)}, u32[]{:S(2)}, u32[]{:S(2)}) %collective-permute-start) | collective-permute-done | bytes 1048608 | tf_op jit(solution)/shard_map/while/body/eval_jaxpr/ppermute | solution.py:20
  312.0 1.3 collective-permute-start
  313.3 35.0 %collective-permute-done = f32[2,2,4,128,128]{4,3,2,0,1:T(8,128)S(1)} collective-permute-done((f32[2,2,4,128,128]{4,3,2,0,1:T(8,128)S(1)}, f32[2,2,4,128,128]{4,3,2,0,1:T(8,128)S(1)}, u32[]{:S(2)}, u32[]{:S(2)}) %collective-permute-start) | collective-permute-done | bytes 1048608 | tf_op jit(solution)/shard_map/while/body/eval_jaxpr/ppermute | solution.py:20
  348.4 1.3 collective-permute-start
  349.7 22.9 %collective-permute-done = f32[2,2,4,128,128]{4,3,2,0,1:T(8,128)S(1)} collective-permute-done((f32[2,2,4,128,128]{4,3,2,0,1:T(8,128)S(1)}, f32[2,2,4,128,128]{4,3,2,0,1:T(8,128)S(1)}, u32[]{:S(2)}, u32[]{:S(2)}) %collective-permute-start) | collective-permute-done | bytes 1048608 | tf_op jit(solution)/shard_map/while/body/eval_jaxpr/ppermute | solution.py:20
  372.8 1.3 collective-permute-start
  374.1 33.1 %collective-permute-done = f32[2,2,4,128,128]{4,3,2,0,1:T(8,128)S(1)} collective-permute-done((f32[2,2,4,128,128]{4,3,2,0,1:T(8,128)S(1)}, f32[2,2,4,128,128]{4,3,2,0,1:T(8,128)S(1)}, u32[]{:S(2)}, u32[]{:S(2)}) %collective-permute-start) | collective-permute-done | bytes 1048608 | tf_op jit(solution)/shard_map/while/body/eval_jaxpr/ppermute | solution.py:20
  407.3 1.3 collective-permute-start
  408.6 71.8 %collective-permute-done = f32[2,2,4,128,128]{4,3,2,0,1:T(8,128)S(1)} collective-permute-done((f32[2,2,4,128,128]{4,3,2,0,1:T(8,128)S(1)}, f32[2,2,4,128,128]{4,3,2,0,1:T(8,128)S(1)}, u32[]{:S(2)}, u32[]{:S(2)}) %collective-permute-start) | collective-permute-done | bytes 1048608 | tf_op jit(solution)/shard_map/while/body/eval_jaxpr/ppermute | solution.py:20
  480.4 12.9 %conditional.7 = (f32[2,4,128,128]{3,2,1,0:T(8,128)}, f32[2,2,128,128]{3,2,1,0:T(8,128)}) conditional(s32[]{:T(128)} %convert_element_type.91, (f32[2,2,128,128]{3,2,0,1:T(8,128)}, f32[2,4,128,128]{3,2,1,0:T(8,128)}) %tuple.96, (f32[2,2,4,128,128]{3,4,2,0,1:T(8,128)}, s32[]{:T(128)}, f32[2,2,4,128,128]{4,3,2,0,1:T(8,128)}, ...), branch_computations={%region_16.17_spmd, %region_17.21_spmd} | conditional | flops 1613824000 | bytes 28835894 | solution.py:158
  480.6 1.6 copy.55
  483.7 1.0 fusion.102
  487.9 1.6 copy.54
  489.5 1.1 add_reduce_fusion.1
  491.4 1.9 add.236
  493.3 1.9 broadcast_select_fusion.5
  495.3 623.5 %all-reduce.3.cloned.1.call-done = f32[2,4,128,128]{3,2,1,0:T(8,128)} async-done(((f32[2,4,128,128]{3,2,1,0:T(8,128)}), f32[2,4,128,128]{3,2,1,0:T(8,128)}) %all-reduce.3.cloned.1.call-update) | async-done | bytes 524304 | tf_op jit(solution)/shard_map/psum | solution.py:192
  1118.8 1.9 broadcast_select_fusion.4
  1120.7 16.7 %while.51 = (s32[]{:T(128)}, f32[2,256,256]{2,1,0:T(8,128)S(1)}, s32[2]{0:T(128)S(1)}, s32[2]{0:T(128)S(1)}, f32[2,2,128,128]{3,2,1,0:T(8,128)}, /*index=5*/s32[]{:T(128)}, s32[]{:T(128)}, s32[]{:T(128)}) while((s32[]{:T(128)}, f32[2,256,256]{2,1,0:T(8,128)S(1)}, s32[2]{0:T(128)S(1)}, s32[2]{0:T(128)S(1)}, f32[2,2,128,128]{3,2,1,0:T(8,128)}, ...), condition=%wide.region_22.23_spmd, body=%wide.region_21.22_spmd.sunk | while | flops 32776 | bytes 655553 | solution.py:184
  1125.8 1.0 bitcast_add_fusion.2
  1126.8 2.3 dynamic_update_slice.8
  1134.2 1.0 bitcast_add_fusion.2
  1135.2 2.2 dynamic_update_slice.8
  1137.5 3.4 collective-permute-start.3
  1140.8 3.3 collective-permute-done.3
  1144.9 55.6 %all-reduce.5.cloned.1.call-done = f32[2,4,128,128]{3,2,1,0:T(8,128)} async-done(((f32[2,4,128,128]{3,2,1,0:T(8,128)}), f32[2,4,128,128]{3,2,1,0:T(8,128)}) %all-reduce.5.cloned.1.call-update) | async-done | bytes 524304 | tf_op jit(solution)/shard_map/psum | solution.py:25
  1200.5 1.5 dynamic-slice_multiply_fusion
  (100 shorter events, 25.7 us)
Async XLA Ops:
  7.2 1111.6 %all-reduce.3.cloned.1.call-start = ((), (), s32[]{:S(2)}) async-start(), calls=%async_computation | async-start | bytes 1048576 | tf_op jit(solution)/shard_map/psum | solution.py:192
  7.2 12.2 %collective-permute-start.2 = (f32[2,1,128,256]{3,2,0,1:T(8,128)}, f32[2,1,128,256]{3,2,0,1:T(8,128)S(1)}, u32[]{:S(2)}, u32[]{:S(2)}) collective-permute-start(f32[2,1,128,256]{3,2,0,1:T(8,128)} %bitcast.391), channel_id=1, source_target_pairs={{0,504},{8,0},{16,8},{24,16},{32,24},{40,32},{48,40},{56,48},{64,5... | collective-permute-start | bytes 786440 | tf_op jit(solution)/shard_map/ppermute | solution.py:14
  17.0 1.7 copy-start.6
  17.6 0.7 copy-start.9
  17.6 0.7 copy-start.10
  18.9 1.0 copy-start.7
  24.0 0.7 copy-start.3
  42.0 17.7 %collective-permute-start.1 = (f32[2,2,4,128,128]{4,3,2,0,1:T(8,128)S(1)}, f32[2,2,4,128,128]{4,3,2,0,1:T(8,128)S(1)}, u32[]{:S(2)}, u32[]{:S(2)}) collective-permute-start(f32[2,2,4,128,128]{4,3,2,0,1:T(8,128)S(1)} %get-tuple-element.1046), channel_id=1, source_target_pairs={{0,1},{1,2},{2,3},{3,4},{4,5},{5,6},{6,7},{8,9},{9,10},{10,11},{11... | collective-permute-start | bytes 3145736 | tf_op jit(solution)/shard_map/while/body/eval_jaxpr/ppermute | solution.py:20
  59.8 34.4 %collective-permute-start.1 = (f32[2,2,4,128,128]{4,3,2,0,1:T(8,128)S(1)}, f32[2,2,4,128,128]{4,3,2,0,1:T(8,128)S(1)}, u32[]{:S(2)}, u32[]{:S(2)}) collective-permute-start(f32[2,2,4,128,128]{4,3,2,0,1:T(8,128)S(1)} %get-tuple-element.1046), channel_id=1, source_target_pairs={{0,1},{1,2},{2,3},{3,4},{4,5},{5,6},{6,7},{8,9},{9,10},{10,11},{11... | collective-permute-start | bytes 3145736 | tf_op jit(solution)/shard_map/while/body/eval_jaxpr/ppermute | solution.py:20
  94.3 21.5 %collective-permute-start.1 = (f32[2,2,4,128,128]{4,3,2,0,1:T(8,128)S(1)}, f32[2,2,4,128,128]{4,3,2,0,1:T(8,128)S(1)}, u32[]{:S(2)}, u32[]{:S(2)}) collective-permute-start(f32[2,2,4,128,128]{4,3,2,0,1:T(8,128)S(1)} %get-tuple-element.1046), channel_id=1, source_target_pairs={{0,1},{1,2},{2,3},{3,4},{4,5},{5,6},{6,7},{8,9},{9,10},{10,11},{11... | collective-permute-start | bytes 3145736 | tf_op jit(solution)/shard_map/while/body/eval_jaxpr/ppermute | solution.py:20
  115.9 26.2 %collective-permute-start.1 = (f32[2,2,4,128,128]{4,3,2,0,1:T(8,128)S(1)}, f32[2,2,4,128,128]{4,3,2,0,1:T(8,128)S(1)}, u32[]{:S(2)}, u32[]{:S(2)}) collective-permute-start(f32[2,2,4,128,128]{4,3,2,0,1:T(8,128)S(1)} %get-tuple-element.1046), channel_id=1, source_target_pairs={{0,1},{1,2},{2,3},{3,4},{4,5},{5,6},{6,7},{8,9},{9,10},{10,11},{11... | collective-permute-start | bytes 3145736 | tf_op jit(solution)/shard_map/while/body/eval_jaxpr/ppermute | solution.py:20
  142.2 26.8 %collective-permute-start.1 = (f32[2,2,4,128,128]{4,3,2,0,1:T(8,128)S(1)}, f32[2,2,4,128,128]{4,3,2,0,1:T(8,128)S(1)}, u32[]{:S(2)}, u32[]{:S(2)}) collective-permute-start(f32[2,2,4,128,128]{4,3,2,0,1:T(8,128)S(1)} %get-tuple-element.1046), channel_id=1, source_target_pairs={{0,1},{1,2},{2,3},{3,4},{4,5},{5,6},{6,7},{8,9},{9,10},{10,11},{11... | collective-permute-start | bytes 3145736 | tf_op jit(solution)/shard_map/while/body/eval_jaxpr/ppermute | solution.py:20
  169.1 20.2 %collective-permute-start.1 = (f32[2,2,4,128,128]{4,3,2,0,1:T(8,128)S(1)}, f32[2,2,4,128,128]{4,3,2,0,1:T(8,128)S(1)}, u32[]{:S(2)}, u32[]{:S(2)}) collective-permute-start(f32[2,2,4,128,128]{4,3,2,0,1:T(8,128)S(1)} %get-tuple-element.1046), channel_id=1, source_target_pairs={{0,1},{1,2},{2,3},{3,4},{4,5},{5,6},{6,7},{8,9},{9,10},{10,11},{11... | collective-permute-start | bytes 3145736 | tf_op jit(solution)/shard_map/while/body/eval_jaxpr/ppermute | solution.py:20
  189.4 32.1 %collective-permute-start.1 = (f32[2,2,4,128,128]{4,3,2,0,1:T(8,128)S(1)}, f32[2,2,4,128,128]{4,3,2,0,1:T(8,128)S(1)}, u32[]{:S(2)}, u32[]{:S(2)}) collective-permute-start(f32[2,2,4,128,128]{4,3,2,0,1:T(8,128)S(1)} %get-tuple-element.1046), channel_id=1, source_target_pairs={{0,1},{1,2},{2,3},{3,4},{4,5},{5,6},{6,7},{8,9},{9,10},{10,11},{11... | collective-permute-start | bytes 3145736 | tf_op jit(solution)/shard_map/while/body/eval_jaxpr/ppermute | solution.py:20
  221.5 16.5 %copy-start.8 = (f32[2,128,128]{2,1,0:T(8,128)S(1)}, f32[2,128,128]{2,1,0:T(8,128)}, u32[]{:S(2)}) copy-start(f32[2,128,128]{2,1,0:T(8,128)} %param.23) | copy-start | bytes 393220
  238.0 1.0 copy-start
  239.3 1.0 copy-start.2
  242.1 16.9 %collective-permute-start = (f32[2,2,4,128,128]{4,3,2,0,1:T(8,128)S(1)}, f32[2,2,4,128,128]{4,3,2,0,1:T(8,128)S(1)}, u32[]{:S(2)}, u32[]{:S(2)}) collective-permute-start(f32[2,2,4,128,128]{4,3,2,0,1:T(8,128)S(1)} %get-tuple-element.1023), channel_id=1, source_target_pairs={{1,0},{2,1},{3,2},{4,3},{5,4},{6,5},{7,6},{9,8},{10,9},{11,10},{12... | collective-permute-start | bytes 3145736 | tf_op jit(solution)/shard_map/while/body/eval_jaxpr/ppermute | solution.py:20
  259.1 29.0 %collective-permute-start = (f32[2,2,4,128,128]{4,3,2,0,1:T(8,128)S(1)}, f32[2,2,4,128,128]{4,3,2,0,1:T(8,128)S(1)}, u32[]{:S(2)}, u32[]{:S(2)}) collective-permute-start(f32[2,2,4,128,128]{4,3,2,0,1:T(8,128)S(1)} %get-tuple-element.1023), channel_id=1, source_target_pairs={{1,0},{2,1},{3,2},{4,3},{5,4},{6,5},{7,6},{9,8},{10,9},{11,10},{12... | collective-permute-start | bytes 3145736 | tf_op jit(solution)/shard_map/while/body/eval_jaxpr/ppermute | solution.py:20
  288.3 23.7 %collective-permute-start = (f32[2,2,4,128,128]{4,3,2,0,1:T(8,128)S(1)}, f32[2,2,4,128,128]{4,3,2,0,1:T(8,128)S(1)}, u32[]{:S(2)}, u32[]{:S(2)}) collective-permute-start(f32[2,2,4,128,128]{4,3,2,0,1:T(8,128)S(1)} %get-tuple-element.1023), channel_id=1, source_target_pairs={{1,0},{2,1},{3,2},{4,3},{5,4},{6,5},{7,6},{9,8},{10,9},{11,10},{12... | collective-permute-start | bytes 3145736 | tf_op jit(solution)/shard_map/while/body/eval_jaxpr/ppermute | solution.py:20
  312.0 36.3 %collective-permute-start = (f32[2,2,4,128,128]{4,3,2,0,1:T(8,128)S(1)}, f32[2,2,4,128,128]{4,3,2,0,1:T(8,128)S(1)}, u32[]{:S(2)}, u32[]{:S(2)}) collective-permute-start(f32[2,2,4,128,128]{4,3,2,0,1:T(8,128)S(1)} %get-tuple-element.1023), channel_id=1, source_target_pairs={{1,0},{2,1},{3,2},{4,3},{5,4},{6,5},{7,6},{9,8},{10,9},{11,10},{12... | collective-permute-start | bytes 3145736 | tf_op jit(solution)/shard_map/while/body/eval_jaxpr/ppermute | solution.py:20
  348.4 24.2 %collective-permute-start = (f32[2,2,4,128,128]{4,3,2,0,1:T(8,128)S(1)}, f32[2,2,4,128,128]{4,3,2,0,1:T(8,128)S(1)}, u32[]{:S(2)}, u32[]{:S(2)}) collective-permute-start(f32[2,2,4,128,128]{4,3,2,0,1:T(8,128)S(1)} %get-tuple-element.1023), channel_id=1, source_target_pairs={{1,0},{2,1},{3,2},{4,3},{5,4},{6,5},{7,6},{9,8},{10,9},{11,10},{12... | collective-permute-start | bytes 3145736 | tf_op jit(solution)/shard_map/while/body/eval_jaxpr/ppermute | solution.py:20
  372.8 34.4 %collective-permute-start = (f32[2,2,4,128,128]{4,3,2,0,1:T(8,128)S(1)}, f32[2,2,4,128,128]{4,3,2,0,1:T(8,128)S(1)}, u32[]{:S(2)}, u32[]{:S(2)}) collective-permute-start(f32[2,2,4,128,128]{4,3,2,0,1:T(8,128)S(1)} %get-tuple-element.1023), channel_id=1, source_target_pairs={{1,0},{2,1},{3,2},{4,3},{5,4},{6,5},{7,6},{9,8},{10,9},{11,10},{12... | collective-permute-start | bytes 3145736 | tf_op jit(solution)/shard_map/while/body/eval_jaxpr/ppermute | solution.py:20
  407.3 73.1 %collective-permute-start = (f32[2,2,4,128,128]{4,3,2,0,1:T(8,128)S(1)}, f32[2,2,4,128,128]{4,3,2,0,1:T(8,128)S(1)}, u32[]{:S(2)}, u32[]{:S(2)}) collective-permute-start(f32[2,2,4,128,128]{4,3,2,0,1:T(8,128)S(1)} %get-tuple-element.1023), channel_id=1, source_target_pairs={{1,0},{2,1},{3,2},{4,3},{5,4},{6,5},{7,6},{9,8},{10,9},{11,10},{12... | collective-permute-start | bytes 3145736 | tf_op jit(solution)/shard_map/while/body/eval_jaxpr/ppermute | solution.py:20
  486.9 1.0 copy-start.5
  495.2 705.3 %all-reduce.5.cloned.1.call-start = ((), (), s32[]{:S(2)}) async-start(), calls=%async_computation.1 | async-start | bytes 1048576 | tf_op jit(solution)/shard_map/psum | solution.py:25
  1137.5 6.7 collective-permute-start.3
Sparse Core Ops, SparseCore 0:
  495.3 623.4 all-reduce.2
  1122.0 78.4 all-reduce.4
where the time goes:
time: 1220 us; the launch traced here: 1210 us
  waiting for transfers between devices  1020 us (84%)
  starting transfers between devices  94.1 us (8%)
  local copies, waits for them, and re-layouts  27.5 us (2%)
  loops' own time  24 us (2%)
  matrix products  19.4 us (2%)
  between operations  14.5 us (1%)
  other arithmetic  12.7 us (1%)
    psum x1, waiting for transfers between devices, per_device(): tile_total = lax.psum(own_probe, 'tile')  624 us
    ppermute x14, waiting for transfers between devices, passed_along(): return lax.ppermute(block, axis, route)  334 us
    ppermute x14, starting transfers between devices, passed_along(): return lax.ppermute(block, axis, route)  81.9 us
    psum x1, waiting for transfers between devices, from_root(): return lax.psum(kept, axis)  55.6 us
  transfers between devices with their start and end apart: 18, of which 17 were waited for; matrix products, arithmetic and copies ran while one was open for 1% of the time, Pallas kernels for 0%

commit v1 on v0

v1 whole, which is shorter than its diff:
```python
import functools
import math

import jax
import jax.numpy as jnp
import ml_dtypes
import numpy as np
from jax import lax
from jax.experimental import pallas as pl
from jax.experimental.pallas import tpu as pltpu
from jax.sharding import PartitionSpec as P

PHASE_RATE = 0.05
SUBLANES = 8
AXES = ("tile", "sec")
POSITION_BIT, CORE_BIT, Z_BITS, X_BIT = 2, 3, (4, 5, 6, 7), 8


def optics(size):
    index = np.arange(size, dtype=np.int32)
    product = index[:, None] * index[None, :] % size
    angle = product.astype(np.float32) * np.float32(2.0 * math.pi / size)
    norm_scale = np.float32(1.0 / math.sqrt(size))
    four = np.cos(angle) * norm_scale - 1j * (np.sin(angle) * norm_scale)
    freq = (index + size // 2) % size - size // 2
    phase = (freq * freq).astype(np.float32) * np.float32(PHASE_RATE)
    kern = np.cos(phase.astype(np.float64)) - 1j * np.sin(phase.astype(np.float64))
    prop = np.conj(four) @ (kern[:, None] * four)
    return four, prop


def as_real(matrix):
    return np.block([[matrix.real, -matrix.imag], [matrix.imag, matrix.real]]).astype(np.float32)


def halves_of(matrix):
    high = matrix.astype(ml_dtypes.bfloat16)
    low = (matrix - high.astype(np.float32)).astype(ml_dtypes.bfloat16)
    return high, low


def tables(size):
    found = []
    for matrix in reversed(optics(size)):
        real = as_real(matrix)
        for one in (real, np.ascontiguousarray(real.T)):
            found.extend(halves_of(one))
    return found


def split(value):
    high = value.astype(jnp.bfloat16)
    low = (value - high.astype(jnp.float32)).astype(jnp.bfloat16)
    return high, low


def dot(left, right):
    return jnp.dot(left, right, preferred_element_type=jnp.float32)


def sandwich(left, right, fields):
    size = fields[0][0].shape[0]
    stacked = jnp.concatenate([jnp.concatenate(pair, axis=0) for pair in fields], axis=1)
    high, low = split(stacked)
    half = dot(left[0][...], high) + (dot(left[0][...], low) + dot(left[1][...], high))
    blocks = [half[:, k * size : (k + 1) * size] for k in range(len(fields))]
    half = jnp.concatenate(
        [jnp.concatenate([b[:size], b[size:]], axis=1) for b in blocks], axis=0
    )
    high, low = split(half)
    out = dot(high, right[0][...]) + (dot(low, right[0][...]) + dot(high, right[1][...]))
    rows = [out[k * size : (k + 1) * size] for k in range(len(fields))]
    return [(row[:, :size], row[:, size:]) for row in rows]


def wave_kernel(
    sec_ref,
    windows,
    probe,
    measured,
    prop_high,
    prop_low,
    back_high,
    back_low,
    four_high,
    four_low,
    inv_high,
    inv_low,
    own_grad,
    sent_grad,
    probe_bands,
    waves,
    grads,
    window_grads,
    probe_grad,
):
    slices = windows.shape[0]
    modes = probe.shape[1]
    size = probe.shape[-1]
    prop, back = (prop_high, prop_low), (back_high, back_low)
    four, inv = (four_high, four_low), (inv_high, inv_low)
    sec = sec_ref[0]
    half_secs = slices // 2
    waves[0] = probe[...]

    def exits(step):
        win_re, win_im = windows[step, 0], windows[step, 1]
        found = []
        for k in range(modes):
            wave_re, wave_im = waves[step, 0, k], waves[step, 1, k]
            found.append((wave_re * win_re - wave_im * win_im, wave_re * win_im + wave_im * win_re))
        return found

    def forward(step, carry):
        for k, (out_re, out_im) in enumerate(sandwich(prop, back, exits(step))):
            waves[step + 1, 0, k] = out_re
            waves[step + 1, 1, k] = out_im
        return carry

    lax.fori_loop(0, slices - 1, forward, 0)
    far = sandwich(four, inv, exits(slices - 1))
    intensity = sum(re * re + im * im for re, im in far)
    weight = 2.0 * (intensity - measured[sec // half_secs])
    for k, (re, im) in enumerate(sandwich(inv, four, [(weight * re, weight * im) for re, im in far])):
        grads[0, k] = re
        grads[1, k] = im

    def window_grad(step):
        total_re = total_im = 0.0
        for k in range(modes):
            wave_re, wave_im = waves[step, 0, k], waves[step, 1, k]
            grad_re, grad_im = grads[0, k], grads[1, k]
            total_re = total_re + (wave_re * grad_re + wave_im * grad_im)
            total_im = total_im + (wave_re * grad_im - wave_im * grad_re)
        window_grads[step, 0] = total_re
        window_grads[step, 1] = total_im

    def entering(step):
        win_re, win_im = windows[step, 0], windows[step, 1]
        found = []
        for k in range(modes):
            grad_re, grad_im = grads[0, k], grads[1, k]
            found.append((win_re * grad_re + win_im * grad_im, win_re * grad_im - win_im * grad_re))
        return found

    def backward(count, carry):
        step = slices - 1 - count
        window_grad(step)
        for k, (re, im) in enumerate(sandwich(back, prop, entering(step))):
            grads[0, k] = re
            grads[1, k] = im
        return carry

    lax.fori_loop(0, slices - 1, backward, 0)
    window_grad(0)
    for k, (re, im) in enumerate(entering(0)):
        probe_grad[k] = re
        probe_grad[modes + k] = im
    own_grad[...] = window_grads[sec]
    partner = lax.rem(sec + half_secs, slices)
    sent_grad[...] = window_grads[partner]
    band = size // slices
    for position in range(2):
        first = (position * half_secs + lax.rem(sec, half_secs)) * band
        probe_bands[position] = probe_grad[:, pl.ds(pl.multiple_of(first, band), band), :]


def aligned(row, size):
    over = lax.rem(row, SUBLANES)
    return pl.multiple_of(row - over, SUBLANES), over, size + SUBLANES


def cut_kernel(row_ref, col_ref, obj, rim, cut, extended):
    own_rows = obj.shape[1]
    size = cut.shape[-1]
    secs = cut.shape[0]
    cols = obj.shape[2]
    count = row_ref.shape[0]
    extended[:, :own_rows] = obj[...]
    extended[:, own_rows:] = rim[...]
    for position in range(count):
        row, col = row_ref[position], col_ref[position]
        base, over, taken = aligned(row, size)
        shift = lax.rem(cols - col, cols)
        for part in range(2):
            rows = extended[part, pl.ds(base, taken), :]
            rows = pltpu.roll(rows, lax.rem(taken - over, taken), 0)[:size]
            window = pltpu.roll(rows, shift, 1)[:, :size]
            for sec in range(position * secs // count, (position + 1) * secs // count):
                cut[sec, part] = window


def scatter_kernel(sec_ref, row_ref, col_ref, own_grad, other_grad, owned, spill, grid):
    rows = owned.shape[1]
    cols = owned.shape[2]
    size = own_grad.shape[-1]
    own = sec_ref[0] // (sec_ref[1] // 2)
    grid[...] = jnp.zeros_like(grid)
    for source, position in ((own_grad, own), (other_grad, 1 - own)):
        row, col = row_ref[position], col_ref[position]
        base, over, taken = aligned(row, size)
        for part in range(2):
            wide = jnp.concatenate([source[part], jnp.zeros((size, cols - size), jnp.float32)], axis=1)
            tall = jnp.concatenate([pltpu.roll(wide, col, 1), jnp.zeros((taken - size, cols), jnp.float32)], axis=0)
            grid[part, pl.ds(base, taken), :] += pltpu.roll(tall, over, 0)
    owned[...] = grid[:, :rows]
    spill[...] = grid[:, rows:]


def groups_of(bits, total):
    rest = [bit for bit in range(total) if bit not in bits]
    found = []
    for r in range(1 << len(rest)):
        base = sum(((r >> i) & 1) << bit for i, bit in enumerate(rest))
        found.append([base + sum(((m >> i) & 1) << bit for i, bit in enumerate(bits)) for m in range(1 << len(bits))])
    return found


def exchanged(blocks, bits):
    total = (lax.axis_size("tile") * lax.axis_size("sec")).bit_length() - 1
    return lax.all_to_all(blocks, AXES, 0, 0, axis_index_groups=groups_of(bits, total))


def per_device(obj, probe, measured, row_offset, col_offset):
    size = probe.shape[-1]
    modes = probe.shape[1]
    rows, cols = obj.shape[2:]
    secs, tiles = lax.axis_size("sec"), lax.axis_size("tile")
    sec = lax.axis_index("sec")
    f32 = jnp.float32
    vmem = pl.BlockSpec(memory_space=pltpu.VMEM)
    smem = pl.BlockSpec(memory_space=pltpu.SMEM)
    params = pltpu.CompilerParams(vmem_limit_bytes=48 * 1024 * 1024)

    own = obj[:, 0]
    rim = lax.ppermute(own, "tile", [(i, (i - 1) % tiles) for i in range(tiles)])
    cut = pl.pallas_call(
        cut_kernel,
        out_shape=jax.ShapeDtypeStruct((secs, 2, size, size), f32),
        in_specs=[smem, smem, vmem, vmem],
        out_specs=vmem,
        scratch_shapes=[pltpu.VMEM((2, 2 * rows, cols), f32)],
        compiler_params=params,
        name="cut_windows",
    )(row_offset, col_offset, own, rim)
    windows = lax.all_to_all(cut, "sec", 0, 0)

    constants = [jnp.asarray(table) for table in tables(size)]
    band = size // secs
    own_grad, sent_grad, bands = pl.pallas_call(
        wave_kernel,
        out_shape=(
            jax.ShapeDtypeStruct((2, size, size), f32),
            jax.ShapeDtypeStruct((2, size, size), f32),
            jax.ShapeDtypeStruct((2, 2 * modes, band, size), f32),
        ),
        in_specs=[smem] + [vmem] * (3 + len(constants)),
        out_specs=(vmem, vmem, vmem),
        scratch_shapes=[
            pltpu.VMEM((secs, 2, modes, size, size), f32),
            pltpu.VMEM((2, modes, size, size), f32),
            pltpu.VMEM((secs, 2, size, size), f32),
            pltpu.VMEM((2 * modes, size, size), f32),
        ],
        compiler_params=params,
        name="wave_gradients",
    )(sec[None], windows, probe, measured, *constants)

    half = secs // 2
    other_grad = lax.ppermute(sent_grad, "sec", [(i, (i + half) % secs) for i in range(secs)])

    near = (CORE_BIT, Z_BITS[0], X_BIT)
    arrived = exchanged(bands.reshape(-1, band, size), near + (POSITION_BIT,))
    part = jnp.sum(arrived, axis=0)

    owned, spill = pl.pallas_call(
        scatter_kernel,
        out_shape=(
            jax.ShapeDtypeStruct((2, rows, cols), f32),
            jax.ShapeDtypeStruct((2, rows, cols), f32),
        ),
        in_specs=[smem, smem, smem, vmem, vmem],
        out_specs=(vmem, vmem),
        scratch_shapes=[pltpu.VMEM((2, 2 * rows, cols), f32)],
        compiler_params=params,
        name="scatter_windows",
    )(jnp.stack([sec, jnp.int32(secs)]), row_offset, col_offset, own_grad, other_grad)
    received = lax.ppermute(spill, "tile", [(i, (i + 1) % tiles) for i in range(tiles)])

    far_bits = Z_BITS[1:]
    part = jnp.sum(exchanged(jnp.broadcast_to(part, (1 << len(far_bits),) + part.shape), far_bits), axis=0)
    pieces = exchanged(jnp.broadcast_to(part, (1 << len(near),) + part.shape), near)
    obj_grad = (owned + received)[:, None]
    probe_grad = pieces.reshape(2, modes, band, size) * (1.0 / (measured.shape[0] * tiles))
    return (obj_grad, probe_grad)


def solution(mesh):
    return jax.shard_map(
        per_device,
        mesh=mesh,
        in_specs=(P(None, "sec", "tile", None), P(), P("tile", None, None), P("tile"), P("tile")),
        out_specs=(P(None, "sec", "tile", None), P(None, None, "sec", None)),
        check_vma=False,
    )
```

time: 1220 us -> 104 us (0.09)
  waiting for transfers between devices: 1020 us -> 19.7 us
  starting transfers between devices: 94.1 us -> 39 us
  local copies, waits for them, and re-layouts: 27.5 us -> 1.66 us
  blocking collectives: 0 us -> 24.9 us
  loops' own time: 24 us -> 0 us
  matrix products: 19.4 us -> 0 us
  Pallas kernels: 0 us -> 16.4 us
  between operations: 14.5 us -> 0.83 us
    psum x2 -> x0, waiting for transfers between devices: 679 us -> none  [the longest x1 624 us: per_device(): tile_total = lax.psum(own_probe, 'tile')]
    ppermute x16 -> x3, waiting for transfers between devices: 338 us -> 5.35 us  [the longest x1 4 us: per_device(): lax.ppermute(sent_grad, 'sec', [(i, (i + half) % secs) for i in range(sec...]
    ppermute x16 -> x3, starting transfers between devices: 94 us -> 15.8 us  [the longest x1 8.92 us: per_device(): lax.ppermute(own, 'tile', [(i, (i - 1) % tiles) for i in range(tiles)])]
    all_to_all x0 -> x1, blocking collectives: none -> 24.9 us  [exchanged(): lax.all_to_all(blocks, AXES, 0, 0, axis_index_groups=groups_of(bits, total))]
    another operation x21 -> x0, loops' own time: 24 us -> none  [the longest x8 15.1 us: forward_work(): return lax.cond(is_live, work, forward_skip_work, (stored, final, incoming))]
    all_to_all x0 -> x3, starting transfers between devices: none -> 23.2 us  [the longest x2 18.9 us: exchanged(): lax.all_to_all(blocks, AXES, 0, 0, axis_index_groups=groups_of(bits, total))]
    dot_general x20 -> x0, matrix products: 19.4 us -> none  [the longest x8 9.4 us: left_mult(): return jnp.einsum('ab,...bc->...ac', matrix, field, precision=HIGH)]
    pallas_call x0 -> x3, Pallas kernels: none -> 16.4 us  [the longest x1 13.7 us: per_device(): pl.pallas_call(wave_kernel, out_shape=(jax.ShapeDtypeStruct((2, size, siz...]
  transfers between devices with their start and end apart: 18 -> 6, of which waited for: 17 -> 4; matrix products, arithmetic and copies ran while one was open for 1% -> 1% of each run, Pallas kernels for 0% -> 1%
where the time goes in v1:
time: 104 us
  starting transfers between devices  39 us (38%)
  blocking collectives  24.9 us (24%)
  waiting for transfers between devices  19.7 us (19%)
  Pallas kernels  16.4 us (16%)
  local copies, waits for them, and re-layouts  1.66 us (2%)
  other arithmetic  1.48 us (1%)
    all_to_all x1, blocking collectives, exchanged(): lax.all_to_all(blocks, AXES, 0, 0, axis_index_groups=groups_of(bits, total))  24.9 us
    all_to_all x2, starting transfers between devices, exchanged(): lax.all_to_all(blocks, AXES, 0, 0, axis_index_groups=groups_of(bits, total))  18.9 us
    pallas_call x1, Pallas kernels, per_device(): pl.pallas_call(wave_kernel, out_shape=(jax.ShapeDtypeStruct((2, size, siz...  13.7 us
    all_to_all x1, waiting for transfers between devices, per_device(): windows = lax.all_to_all(cut, 'sec', 0, 0)  9.45 us
    ppermute x1, starting transfers between devices, per_device(): lax.ppermute(own, 'tile', [(i, (i - 1) % tiles) for i in range(tiles)])  8.92 us
    all_to_all x2, waiting for transfers between devices, exchanged(): lax.all_to_all(blocks, AXES, 0, 0, axis_index_groups=groups_of(bits, total))  4.92 us
    all_to_all x1, starting transfers between devices, per_device(): windows = lax.all_to_all(cut, 'sec', 0, 0)  4.31 us
    ppermute x1, waiting for transfers between devices, per_device(): lax.ppermute(sent_grad, 'sec', [(i, (i + half) % secs) for i in range(sec...  4 us
  transfers between devices with their start and end apart: 6, of which 4 were waited for; matrix products, arithmetic and copies ran while one was open for 1% of the time, Pallas kernels for 1%

profile of v1, /device:TPU:1, one launch (start us, length us, event | category | flops | bytes accessed | tf_op | source)
XLA Modules:
  0.0 103.9 jit_solution(3438679159258893509)
XLA Ops:
  0.6 0.0 copy-start.11
  0.6 0.0 copy-start.12
  0.6 8.9 %collective-permute-start = (f32[2,128,256]{2,1,0:T(8,128)}, f32[2,128,256]{2,1,0:T(8,128)S(1)}, u32[]{:S(2)}, u32[]{:S(2)}) collective-permute-start(f32[2,128,256]{2,1,0:T(8,128)} %bitcast.8), channel_id=1, source_target_pairs={{0,504},{8,0},{16,8},{24,16},{32,24},{40,32},{48,40},{56,48},{64,5... | collective-permute-start | bytes 786440 | tf_op jit(solution)/shard_map/ppermute | solution.py:236
  9.6 1.4 %collective-permute-done.rim = f32[2,128,256]{2,1,0:T(8,128)S(1)} collective-permute-done((f32[2,128,256]{2,1,0:T(8,128)}, f32[2,128,256]{2,1,0:T(8,128)S(1)}, u32[]{:S(2)}, u32[]{:S(2)}) %collective-permute-start) | collective-permute-done | bytes 262176 | tf_op jit(solution)/shard_map/ppermute | solution.py:236
  10.9 0.0 copy-done.11
  10.9 0.0 copy-done.12
  10.9 0.0 copy-start.1
  10.9 0.9 copy-done.1
  11.9 1.8 %cut_windows.1 = f32[8,2,128,128]{3,2,1,0:T(8,128)} custom-call(s32[2]{0:T(128)S(1)} %copy-done.11, s32[2]{0:T(128)S(1)} %copy-done.12, f32[2,128,256]{2,1,0:T(8,128)S(1)} %bitcast.9, f32[2,128,256]{2,1,0:T(8,128)S(1)} %collective-permute-done.rim), custom_call_target="tpu_custom_call" | custom-call | tf_op jit(solution)/shard_map/cut_windows/pallas_call | solution.py:237
  13.7 0.0 copy-start
  13.7 0.0 copy-start.2
  13.7 0.0 copy-start.3
  13.7 0.0 copy-start.4
  13.7 0.0 copy-start.5
  13.7 0.0 copy-start.6
  13.7 0.0 copy-start.7
  13.7 0.0 copy-start.8
  13.7 0.0 copy-start.9
  13.7 0.0 copy-start.10
  13.8 4.3 %all-to-all-start = ((f32[8,2,128,128]{3,2,1,0:T(8,128)}), f32[8,2,128,128]{3,2,1,0:T(8,128)S(1)}, u32[]{:S(2)}, u32[]{:S(2)}) async-start(f32[8,2,128,128]{3,2,1,0:T(8,128)} %cut_windows.1), calls=%async_computation | async-start | bytes 2097152 | tf_op jit(solution)/shard_map/all_to_all | solution.py:246
  18.1 9.4 %all-to-all-done.windows = f32[8,2,128,128]{3,2,1,0:T(8,128)S(1)} async-done(((f32[8,2,128,128]{3,2,1,0:T(8,128)}), f32[8,2,128,128]{3,2,1,0:T(8,128)S(1)}, u32[]{:S(2)}, u32[]{:S(2)}) %all-to-all-start) | async-done | bytes 1048608 | tf_op jit(solution)/shard_map/all_to_all | solution.py:246
  27.5 0.0 copy-done
  27.5 0.0 copy-done.2
  27.5 0.0 copy-done.3
  27.5 0.0 copy-done.4
  27.5 0.0 copy-done.5
  27.5 0.0 copy-done.6
  27.6 0.0 copy-done.7
  27.6 0.0 copy-done.8
  27.6 0.0 copy-done.9
  27.6 0.0 copy-done.10
  27.6 13.7 %wave_gradients.1 = (f32[2,128,128]{2,1,0:T(8,128)S(1)}, f32[2,128,128]{2,1,0:T(8,128)S(1)}, f32[2,8,16,128]{3,2,1,0:T(8,128)}) custom-call(s32[1]{0:T(128)} %bitcast.sec_ref, f32[8,2,128,128]{3,2,1,0:T(8,128)S(1)} %all-to-all-done.windows, f32[2,4,128,128]{3,2,1,0:T(8,128)S(1)} %copy-done, f32[2,128,128]{2,1,0:T(8,128)S(1)} %copy-done.2, ...), custom_call_target="tpu_custom_call" | custom-call | tf_op jit(solution)/shard_map/wave_gradients/pallas_call | solution.py:250
  41.3 13.6 %all-to-all-start.1 = ((f32[16,16,128]{2,1,0:T(8,128)}), f32[16,16,128]{2,1,0:T(8,128)S(1)}, u32[]{:S(2)}, u32[]{:S(2)}) async-start(f32[16,16,128]{2,1,0:T(8,128)} %bitcast.4), calls=%async_computation.1 | async-start | bytes 262144 | tf_op jit(solution)/shard_map/all_to_all | solution.py:221
  54.9 3.3 %collective-permute-start.1 = (f32[2,128,128]{2,1,0:T(8,128)S(1)}, f32[2,128,128]{2,1,0:T(8,128)S(1)}, u32[]{:S(2)}, u32[]{:S(2)}) collective-permute-start(f32[2,128,128]{2,1,0:T(8,128)S(1)} %get-tuple-element.8), channel_id=1, source_target_pairs={{0,4},{1,5},{2,6},{3,7},{4,0},{5,1},{6,2},{7,3},{8,12},{9,13},{10,... | collective-permute-start | bytes 393224 | tf_op jit(solution)/shard_map/ppermute | solution.py:270
  58.3 0.1 pad_add_fusion.sec_ref
  58.3 4.0 %collective-permute-done.1.other_grad = f32[2,128,128]{2,1,0:T(8,128)S(1)} collective-permute-done((f32[2,128,128]{2,1,0:T(8,128)S(1)}, f32[2,128,128]{2,1,0:T(8,128)S(1)}, u32[]{:S(2)}, u32[]{:S(2)}) %collective-permute-start.1) | collective-permute-done | bytes 131104 | tf_op jit(solution)/shard_map/ppermute | solution.py:270
  62.3 0.9 scatter_windows.1
  63.2 3.6 %collective-permute-start.2 = (f32[2,128,256]{2,1,0:T(8,128)S(1)}, f32[2,128,256]{2,1,0:T(8,128)S(1)}, u32[]{:S(2)}, u32[]{:S(2)}) collective-permute-start(f32[2,128,256]{2,1,0:T(8,128)S(1)} %get-tuple-element.10), channel_id=1, source_target_pairs={{0,8},{8,16},{16,24},{24,32},{32,40},{40,48},{48,56},{56,64},{64,7... | collective-permute-start | bytes 786440 | tf_op jit(solution)/shard_map/ppermute | solution.py:288
  66.8 0.0 all-to-all-done.1
  66.8 24.9 %all_to_all.20 = f32[8,16,128]{2,1,0:T(8,128)S(1)} all-to-all(f32[8,16,128]{2,1,0:T(8,128)S(1)} %broadcast_in_dim.11), channel_id=1, replica_groups={{0,32,64,96,128,160,192,224},{1,33,65,97,129,161,193,225},{2,34,66,98,1..., dimensions={0} | all-to-all | bytes 131072 | tf_op jit(solution)/shard_map/all_to_all | solution.py:221
  91.7 0.6 broadcast_in_dim.12
  92.4 5.2 %all-to-all-start.3 = ((f32[8,16,128]{2,1,0:T(8,128)}), f32[8,16,128]{2,1,0:T(8,128)S(1)}, u32[]{:S(2)}, u32[]{:S(2)}) async-start(f32[8,16,128]{2,1,0:T(8,128)} %broadcast_in_dim.12), calls=%async_computation.3 | async-start | bytes 131072 | tf_op jit(solution)/shard_map/all_to_all | solution.py:221
  97.6 0.0 collective-permute-done.2
  97.6 0.7 add_bitcast_fusion
  98.3 4.9 %all-to-all-done.3 = f32[8,16,128]{2,1,0:T(8,128)S(1)} async-done(((f32[8,16,128]{2,1,0:T(8,128)}), f32[8,16,128]{2,1,0:T(8,128)S(1)}, u32[]{:S(2)}, u32[]{:S(2)}) %all-to-all-start.3) | async-done | bytes 65568 | tf_op jit(solution)/shard_map/all_to_all | solution.py:221
  103.3 0.6 broadcast_multiply_fusion
  (3 shorter events, 0.0 us)
Async XLA Ops:
  0.6 10.3 %copy-start.11 = (s32[2]{0:T(128)S(1)}, s32[2]{0:T(128)}, u32[]{:S(2)}) copy-start(s32[2]{0:T(128)} %row_ref.3) | copy-start | bytes 28
  0.6 10.3 %copy-start.12 = (s32[2]{0:T(128)S(1)}, s32[2]{0:T(128)}, u32[]{:S(2)}) copy-start(s32[2]{0:T(128)} %col_ref.3) | copy-start | bytes 28
  0.6 10.3 %collective-permute-start = (f32[2,128,256]{2,1,0:T(8,128)}, f32[2,128,256]{2,1,0:T(8,128)S(1)}, u32[]{:S(2)}, u32[]{:S(2)}) collective-permute-start(f32[2,128,256]{2,1,0:T(8,128)} %bitcast.8), channel_id=1, source_target_pairs={{0,504},{8,0},{16,8},{24,16},{32,24},{40,32},{48,40},{56,48},{64,5... | collective-permute-start | bytes 786440 | tf_op jit(solution)/shard_map/ppermute | solution.py:236
  10.9 1.0 copy-start.1
  13.7 13.9 %copy-start = (f32[2,4,128,128]{3,2,1,0:T(8,128)S(1)}, f32[2,4,128,128]{3,2,1,0:T(8,128)}, u32[]{:S(2)}) copy-start(f32[2,4,128,128]{3,2,1,0:T(8,128)} %probe.1) | copy-start | bytes 1572868
  13.7 13.9 %copy-start.2 = (f32[2,128,128]{2,1,0:T(8,128)S(1)}, f32[2,128,128]{2,1,0:T(8,128)}, u32[]{:S(2)}) copy-start(f32[2,128,128]{2,1,0:T(8,128)} %measured.1) | copy-start | bytes 393220
  13.7 13.9 %copy-start.3 = (bf16[256,256]{1,0:T(8,128)(2,1)S(1)}, bf16[256,256]{1,0:T(8,128)(2,1)}, u32[]{:S(2)}) copy-start(bf16[256,256]{1,0:T(8,128)(2,1)} %constant.26.clone.prop_high) | copy-start | bytes 393220
  13.7 13.9 %copy-start.4 = (bf16[256,256]{1,0:T(8,128)(2,1)S(1)}, bf16[256,256]{1,0:T(8,128)(2,1)}, u32[]{:S(2)}) copy-start(bf16[256,256]{1,0:T(8,128)(2,1)} %constant.27.clone.prop_low) | copy-start | bytes 393220
  13.7 13.9 %copy-start.5 = (bf16[256,256]{1,0:T(8,128)(2,1)S(1)}, bf16[256,256]{1,0:T(8,128)(2,1)}, u32[]{:S(2)}) copy-start(bf16[256,256]{1,0:T(8,128)(2,1)} %constant.28.clone.back_high) | copy-start | bytes 393220
  13.7 13.9 %copy-start.6 = (bf16[256,256]{1,0:T(8,128)(2,1)S(1)}, bf16[256,256]{1,0:T(8,128)(2,1)}, u32[]{:S(2)}) copy-start(bf16[256,256]{1,0:T(8,128)(2,1)} %constant.29.clone.back_low) | copy-start | bytes 393220
  13.7 13.9 %copy-start.7 = (bf16[256,256]{1,0:T(8,128)(2,1)S(1)}, bf16[256,256]{1,0:T(8,128)(2,1)}, u32[]{:S(2)}) copy-start(bf16[256,256]{1,0:T(8,128)(2,1)} %constant.30.clone.four_high) | copy-start | bytes 393220
  13.7 13.9 %copy-start.8 = (bf16[256,256]{1,0:T(8,128)(2,1)S(1)}, bf16[256,256]{1,0:T(8,128)(2,1)}, u32[]{:S(2)}) copy-start(bf16[256,256]{1,0:T(8,128)(2,1)} %constant.31.clone.four_low) | copy-start | bytes 393220
  13.7 13.8 %copy-start.9 = (bf16[256,256]{1,0:T(8,128)(2,1)S(1)}, bf16[256,256]{1,0:T(8,128)(2,1)}, u32[]{:S(2)}) copy-start(bf16[256,256]{1,0:T(8,128)(2,1)} %constant.32.clone.inv_high) | copy-start | bytes 393220
  13.7 13.8 %copy-start.10 = (bf16[256,256]{1,0:T(8,128)(2,1)S(1)}, bf16[256,256]{1,0:T(8,128)(2,1)}, u32[]{:S(2)}) copy-start(bf16[256,256]{1,0:T(8,128)(2,1)} %constant.33.clone.inv_low) | copy-start | bytes 393220
  13.8 13.8 %all-to-all-start = ((f32[8,2,128,128]{3,2,1,0:T(8,128)}), f32[8,2,128,128]{3,2,1,0:T(8,128)S(1)}, u32[]{:S(2)}, u32[]{:S(2)}) async-start(f32[8,2,128,128]{3,2,1,0:T(8,128)} %cut_windows.1), calls=%async_computation | async-start | bytes 2097152 | tf_op jit(solution)/shard_map/all_to_all | solution.py:246
  41.3 25.5 %all-to-all-start.1 = ((f32[16,16,128]{2,1,0:T(8,128)}), f32[16,16,128]{2,1,0:T(8,128)S(1)}, u32[]{:S(2)}, u32[]{:S(2)}) async-start(f32[16,16,128]{2,1,0:T(8,128)} %bitcast.4), calls=%async_computation.1 | async-start | bytes 262144 | tf_op jit(solution)/shard_map/all_to_all | solution.py:221
  54.9 7.4 %collective-permute-start.1 = (f32[2,128,128]{2,1,0:T(8,128)S(1)}, f32[2,128,128]{2,1,0:T(8,128)S(1)}, u32[]{:S(2)}, u32[]{:S(2)}) collective-permute-start(f32[2,128,128]{2,1,0:T(8,128)S(1)} %get-tuple-element.8), channel_id=1, source_target_pairs={{0,4},{1,5},{2,6},{3,7},{4,0},{5,1},{6,2},{7,3},{8,12},{9,13},{10,... | collective-permute-start | bytes 393224 | tf_op jit(solution)/shard_map/ppermute | solution.py:270
  63.2 34.4 %collective-permute-start.2 = (f32[2,128,256]{2,1,0:T(8,128)S(1)}, f32[2,128,256]{2,1,0:T(8,128)S(1)}, u32[]{:S(2)}, u32[]{:S(2)}) collective-permute-start(f32[2,128,256]{2,1,0:T(8,128)S(1)} %get-tuple-element.10), channel_id=1, source_target_pairs={{0,8},{8,16},{16,24},{24,32},{32,40},{40,48},{48,56},{56,64},{64,7... | collective-permute-start | bytes 786440 | tf_op jit(solution)/shard_map/ppermute | solution.py:288
  92.4 10.9 %all-to-all-start.3 = ((f32[8,16,128]{2,1,0:T(8,128)}), f32[8,16,128]{2,1,0:T(8,128)S(1)}, u32[]{:S(2)}, u32[]{:S(2)}) async-start(f32[8,16,128]{2,1,0:T(8,128)} %broadcast_in_dim.12), calls=%async_computation.3 | async-start | bytes 131072 | tf_op jit(solution)/shard_map/all_to_all | solution.py:221

commit v2 on v1

--- a/solution.py
+++ b/solution.py
@@ -12,6 +12,7 @@
 
 PHASE_RATE = 0.05
 SUBLANES = 8
+VMEM_BYTES = 48 * 1024 * 1024
 AXES = ("tile", "sec")
 POSITION_BIT, CORE_BIT, Z_BITS, X_BIT = 2, 3, (4, 5, 6, 7), 8
 
@@ -58,22 +59,26 @@
     return jnp.dot(left, right, preferred_element_type=jnp.float32)
 
 
-def sandwich(left, right, fields):
+def flipped(block):
+    size = block.shape[0]
+    return jnp.concatenate([block[:, :size].T, block[:, size:].T], axis=1)
+
+
+def product(halves, right):
+    high, low = halves
+    return dot(high, right[0][...]) + (dot(low, right[0][...]) + dot(high, right[1][...]))
+
+
+def sandwich(right, fields):
+    first = [product(split(jnp.concatenate(pair, axis=1)), right) for pair in fields]
+    turned_over = [tuple(flipped(part) for part in split(half)) for half in first]
+    out = [product(halves, right) for halves in turned_over]
     size = fields[0][0].shape[0]
-    stacked = jnp.concatenate([jnp.concatenate(pair, axis=0) for pair in fields], axis=1)
-    high, low = split(stacked)
-    half = dot(left[0][...], high) + (dot(left[0][...], low) + dot(left[1][...], high))
-    blocks = [half[:, k * size : (k + 1) * size] for k in range(len(fields))]
-    half = jnp.concatenate(
-        [jnp.concatenate([b[:size], b[size:]], axis=1) for b in blocks], axis=0
-    )
-    high, low = split(half)
-    out = dot(high, right[0][...]) + (dot(low, right[0][...]) + dot(high, right[1][...]))
-    rows = [out[k * size : (k + 1) * size] for k in range(len(fields))]
-    return [(row[:, :size], row[:, size:]) for row in rows]
+    return [(field[:, :size], field[:, size:]) for field in out]
 
 
 def wave_kernel(
+    scale,
     sec_ref,
     windows,
     probe,
@@ -111,17 +116,14 @@
             found.append((wave_re * win_re - wave_im * win_im, wave_re * win_im + wave_im * win_re))
         return found
 
-    def forward(step, carry):
-        for k, (out_re, out_im) in enumerate(sandwich(prop, back, exits(step))):
+    for step in range(slices - 1):
+        for k, (out_re, out_im) in enumerate(sandwich(back, exits(step))):
             waves[step + 1, 0, k] = out_re
             waves[step + 1, 1, k] = out_im
-        return carry
-
-    lax.fori_loop(0, slices - 1, forward, 0)
-    far = sandwich(four, inv, exits(slices - 1))
+    far = sandwich(inv, exits(slices - 1))
     intensity = sum(re * re + im * im for re, im in far)
     weight = 2.0 * (intensity - measured[sec // half_secs])
-    for k, (re, im) in enumerate(sandwich(inv, four, [(weight * re, weight * im) for re, im in far])):
+    for k, (re, im) in enumerate(sandwich(four, [(weight * re, weight * im) for re, im in far])):
         grads[0, k] = re
         grads[1, k] = im
 
@@ -132,8 +134,8 @@
             grad_re, grad_im = grads[0, k], grads[1, k]
             total_re = total_re + (wave_re * grad_re + wave_im * grad_im)
             total_im = total_im + (wave_re * grad_im - wave_im * grad_re)
-        window_grads[step, 0] = total_re
-        window_grads[step, 1] = total_im
+        window_grads[step, 0] = total_re.T if step % 2 else total_re
+        window_grads[step, 1] = total_im.T if step % 2 else total_im
 
     def entering(step):
         win_re, win_im = windows[step, 0], windows[step, 1]
@@ -143,19 +145,15 @@
             found.append((win_re * grad_re + win_im * grad_im, win_re * grad_im - win_im * grad_re))
         return found
 
-    def backward(count, carry):
-        step = slices - 1 - count
+    for step in reversed(range(1, slices)):
         window_grad(step)
-        for k, (re, im) in enumerate(sandwich(back, prop, entering(step))):
+        for k, (re, im) in enumerate(sandwich(prop, entering(step))):
             grads[0, k] = re
             grads[1, k] = im
-        return carry
-
-    lax.fori_loop(0, slices - 1, backward, 0)
     window_grad(0)
     for k, (re, im) in enumerate(entering(0)):
-        probe_grad[k] = re
-        probe_grad[modes + k] = im
+        probe_grad[k] = re * scale
+        probe_grad[modes + k] = im * scale
     own_grad[...] = window_grads[sec]
     partner = lax.rem(sec + half_secs, slices)
     sent_grad[...] = window_grads[partner]
@@ -170,22 +168,30 @@
     return pl.multiple_of(row - over, SUBLANES), over, size + SUBLANES
 
 
-def cut_kernel(row_ref, col_ref, obj, rim, cut, extended):
-    own_rows = obj.shape[1]
+def turned(block, row, col, size):
+    rows, cols = block.shape
+    block = pltpu.roll(block, lax.rem(rows - row, rows), 0)
+    return pltpu.roll(block, lax.rem(cols - col, cols), 1)[:, :size]
+
+
+def own_kernel(row_ref, col_ref, obj, out):
+    for position in range(out.shape[0]):
+        for part in range(2):
+            out[position, part] = turned(obj[part], row_ref[position], col_ref[position], out.shape[-1])
+
+
+def cut_kernel(sec_ref, row_ref, col_ref, own, rim, cut):
     size = cut.shape[-1]
     secs = cut.shape[0]
-    cols = obj.shape[2]
-    count = row_ref.shape[0]
-    extended[:, :own_rows] = obj[...]
-    extended[:, own_rows:] = rim[...]
+    count = own.shape[0]
+    odd = lax.rem(sec_ref[0], 2) == 1
+    place = lax.broadcasted_iota(jnp.int32, (size, size), 0)
     for position in range(count):
-        row, col = row_ref[position], col_ref[position]
-        base, over, taken = aligned(row, size)
-        shift = lax.rem(cols - col, cols)
+        row = row_ref[position]
         for part in range(2):
-            rows = extended[part, pl.ds(base, taken), :]
-            rows = pltpu.roll(rows, lax.rem(taken - over, taken), 0)[:size]
-            window = pltpu.roll(rows, shift, 1)[:, :size]
+            beyond = turned(rim[part], row, col_ref[position], size)
+            window = jnp.where(place < size - row, own[position, part], beyond)
+            window = jnp.where(odd, window.T, window)
             for sec in range(position * secs // count, (position + 1) * secs // count):
                 cut[sec, part] = window
 
@@ -221,34 +227,16 @@
     return lax.all_to_all(blocks, AXES, 0, 0, axis_index_groups=groups_of(bits, total))
 
 
-def per_device(obj, probe, measured, row_offset, col_offset):
-    size = probe.shape[-1]
-    modes = probe.shape[1]
-    rows, cols = obj.shape[2:]
-    secs, tiles = lax.axis_size("sec"), lax.axis_size("tile")
-    sec = lax.axis_index("sec")
+def wave_call(sec, windows, probe, measured, positions=128):
+    secs = windows.shape[0]
+    modes, size = probe.shape[1], probe.shape[-1]
     f32 = jnp.float32
     vmem = pl.BlockSpec(memory_space=pltpu.VMEM)
     smem = pl.BlockSpec(memory_space=pltpu.SMEM)
-    params = pltpu.CompilerParams(vmem_limit_bytes=48 * 1024 * 1024)
-
-    own = obj[:, 0]
-    rim = lax.ppermute(own, "tile", [(i, (i - 1) % tiles) for i in range(tiles)])
-    cut = pl.pallas_call(
-        cut_kernel,
-        out_shape=jax.ShapeDtypeStruct((secs, 2, size, size), f32),
-        in_specs=[smem, smem, vmem, vmem],
-        out_specs=vmem,
-        scratch_shapes=[pltpu.VMEM((2, 2 * rows, cols), f32)],
-        compiler_params=params,
-        name="cut_windows",
-    )(row_offset, col_offset, own, rim)
-    windows = lax.all_to_all(cut, "sec", 0, 0)
-
     constants = [jnp.asarray(table) for table in tables(size)]
     band = size // secs
-    own_grad, sent_grad, bands = pl.pallas_call(
-        wave_kernel,
+    return pl.pallas_call(
+        functools.partial(wave_kernel, 1.0 / positions),
         out_shape=(
             jax.ShapeDtypeStruct((2, size, size), f32),
             jax.ShapeDtypeStruct((2, size, size), f32),
@@ -262,16 +250,52 @@
             pltpu.VMEM((secs, 2, size, size), f32),
             pltpu.VMEM((2 * modes, size, size), f32),
         ],
+        compiler_params=pltpu.CompilerParams(vmem_limit_bytes=VMEM_BYTES),
+        name="wave_gradients",
+    )(sec, windows, probe, measured, *constants)
+
+
+def per_device(obj, probe, measured, row_offset, col_offset):
+    size = probe.shape[-1]
+    modes = probe.shape[1]
+    rows, cols = obj.shape[2:]
+    secs, tiles = lax.axis_size("sec"), lax.axis_size("tile")
+    sec = lax.axis_index("sec")
+    f32 = jnp.float32
+    vmem = pl.BlockSpec(memory_space=pltpu.VMEM)
+    smem = pl.BlockSpec(memory_space=pltpu.SMEM)
+    params = pltpu.CompilerParams(vmem_limit_bytes=VMEM_BYTES)
+
+    own = obj[:, 0]
+    rim = lax.ppermute(own, "tile", [(i, (i - 1) % tiles) for i in range(tiles)])
+    own_windows = pl.pallas_call(
+        own_kernel,
+        out_shape=jax.ShapeDtypeStruct((measured.shape[0], 2, size, size), f32),
+        in_specs=[smem, smem, vmem],
+        out_specs=vmem,
         compiler_params=params,
-        name="wave_gradients",
-    )(sec[None], windows, probe, measured, *constants)
-
+        name="own_windows",
+    )(row_offset, col_offset, own)
+    cut = pl.pallas_call(
+        cut_kernel,
+        out_shape=jax.ShapeDtypeStruct((secs, 2, size, size), f32),
+        in_specs=[smem, smem, smem, vmem, vmem],
+        out_specs=vmem,
+        compiler_params=params,
+        name="cut_windows",
+    )(sec[None], row_offset, col_offset, own_windows, rim)
+    windows = lax.all_to_all(cut, "sec", 0, 0)
+
+    own_grad, sent_grad, bands = wave_call(sec[None], windows, probe, measured, measured.shape[0] * tiles)
+
+    band = size // secs
     half = secs // 2
     other_grad = lax.ppermute(sent_grad, "sec", [(i, (i + half) % secs) for i in range(secs)])
 
     near = (CORE_BIT, Z_BITS[0], X_BIT)
     arrived = exchanged(bands.reshape(-1, band, size), near + (POSITION_BIT,))
     part = jnp.sum(arrived, axis=0)
+    other_grad = lax.optimization_barrier((other_grad, part))[0]
 
     owned, spill = pl.pallas_call(
         scatter_kernel,
@@ -285,13 +309,14 @@
         compiler_params=params,
         name="scatter_windows",
     )(jnp.stack([sec, jnp.int32(secs)]), row_offset, col_offset, own_grad, other_grad)
-    received = lax.ppermute(spill, "tile", [(i, (i + 1) % tiles) for i in range(tiles)])
-
     far_bits = Z_BITS[1:]
     part = jnp.sum(exchanged(jnp.broadcast_to(part, (1 << len(far_bits),) + part.shape), far_bits), axis=0)
+    spill = lax.optimization_barrier((spill, part))[0]
+    received = lax.ppermute(spill, "tile", [(i, (i + 1) % tiles) for i in range(tiles)])
+
     pieces = exchanged(jnp.broadcast_to(part, (1 << len(near),) + part.shape), near)
     obj_grad = (owned + received)[:, None]
-    probe_grad = pieces.reshape(2, modes, band, size) * (1.0 / (measured.shape[0] * tiles))
+    probe_grad = pieces.reshape(2, modes, band, size)
     return (obj_grad, probe_grad)
 
 

time: 104 us -> 94.6 us (0.910)
  blocking collectives: 24.9 us -> 41.9 us
  starting transfers between devices: 39 us -> 27 us
  waiting for transfers between devices: 19.7 us -> 9.07 us
  Pallas kernels: 16.4 us -> 11.5 us
  local copies, waits for them, and re-layouts: 1.66 us -> 2.94 us
    all_to_all x0 -> x1, blocking collectives: none -> 13.3 us  [per_device(): windows = lax.all_to_all(cut, 'sec', 0, 0)]
    all_to_all x1 -> x0, waiting for transfers between devices: 9.45 us -> none  [per_device(): windows = lax.all_to_all(cut, 'sec', 0, 0)]
    all_to_all x2 -> x1, starting transfers between devices: 18.9 us -> 11.3 us  [exchanged(): lax.all_to_all(blocks, AXES, 0, 0, axis_index_groups=groups_of(bits, total))]
    all_to_all x1 -> x0, starting transfers between devices: 4.31 us -> none  [per_device(): windows = lax.all_to_all(cut, 'sec', 0, 0)]
    pallas_call x1 -> x2, Pallas kernels: 13.7 us -> 9.7 us  [the longest x1 8.94 us: wave_call(): pl.pallas_call(functools.partial(wave_kernel, 1.0 / positions), out_shape...]
    all_to_all x1 -> x2, blocking collectives: 24.9 us -> 28.6 us  [exchanged(): lax.all_to_all(blocks, AXES, 0, 0, axis_index_groups=groups_of(bits, total))]
    ppermute x1, waiting for transfers between devices: 1.35 us -> 0.01 us  [per_device(): lax.ppermute(own, 'tile', [(i, (i - 1) % tiles) for i in range(tiles)])]
    unnamed x26 -> x27, local copies, waits for them, and re-layouts: 1.01 us -> 2.3 us
  transfers between devices with their start and end apart: 6 -> 4, of which waited for: 4 -> 2; matrix products, arithmetic and copies ran while one was open for 1% -> 0% of each run, Pallas kernels for 1% -> 2%
where the time goes in v2:
time: 94.6 us; the launch traced here: 94.2 us
  blocking collectives  41.9 us (44%)
  starting transfers between devices  27 us (29%)
  Pallas kernels  11.5 us (12%)
  waiting for transfers between devices  9.07 us (10%)
  local copies, waits for them, and re-layouts  2.94 us (3%)
    all_to_all x2, blocking collectives, exchanged(): lax.all_to_all(blocks, AXES, 0, 0, axis_index_groups=groups_of(bits, total))  28.6 us
    all_to_all x1, blocking collectives, per_device(): windows = lax.all_to_all(cut, 'sec', 0, 0)  13.3 us
    all_to_all x1, starting transfers between devices, exchanged(): lax.all_to_all(blocks, AXES, 0, 0, axis_index_groups=groups_of(bits, total))  11.3 us
    pallas_call x1, Pallas kernels, wave_call(): pl.pallas_call(functools.partial(wave_kernel, 1.0 / positions), out_shape...  8.94 us
    ppermute x1, starting transfers between devices, per_device(): lax.ppermute(own, 'tile', [(i, (i - 1) % tiles) for i in range(tiles)])  8.79 us
    all_to_all x1, waiting for transfers between devices, exchanged(): lax.all_to_all(blocks, AXES, 0, 0, axis_index_groups=groups_of(bits, total))  5.29 us
    ppermute x1, starting transfers between devices, per_device(): lax.ppermute(spill, 'tile', [(i, (i + 1) % tiles) for i in range(tiles)])  4.77 us
    ppermute x1, waiting for transfers between devices, per_device(): lax.ppermute(sent_grad, 'sec', [(i, (i + half) % secs) for i in range(sec...  3.77 us
  transfers between devices with their start and end apart: 4, of which 2 were waited for; matrix products, arithmetic and copies ran while one was open for 0% of the time, Pallas kernels for 2%

profile of v2, /device:TPU:1, one launch (start us, length us, event | category | flops | bytes accessed | tf_op | source)
XLA Modules:
  0.0 94.2 jit_solution(9500871039189200057)
XLA Ops:
  0.6 8.8 %collective-permute-start = (f32[2,128,256]{2,1,0:T(8,128)}, f32[2,128,256]{2,1,0:T(8,128)S(1)}, u32[]{:S(2)}, u32[]{:S(2)}) collective-permute-start(f32[2,128,256]{2,1,0:T(8,128)} %bitcast.8), channel_id=1, source_target_pairs={{0,504},{8,0},{16,8},{24,16},{32,24},{40,32},{48,40},{56,48},{64,5... | collective-permute-start | bytes 786440 | tf_op jit(solution)/shard_map/ppermute | solution.py:270
  9.4 0.0 copy-start.11
  9.4 0.0 copy-start.12
  9.4 0.6 copy-done.11
  10.1 0.0 copy-done.12
  10.1 0.0 copy-start.1
  10.1 0.9 %copy-done.1 = f32[2,1,128,256]{3,2,1,0:T(8,128)S(1)} copy-done((f32[2,1,128,256]{3,2,1,0:T(8,128)S(1)}, f32[2,1,128,256]{3,2,1,0:T(8,128)}, u32[]{:S(2)}) %copy-start.1) | copy-done | bytes 262168
  11.1 0.8 own_windows.1.own
  11.8 0.0 collective-permute-done.rim
  11.8 0.9 cut_windows.1
  12.8 0.0 copy-start
  12.8 0.0 copy-start.2
  12.8 0.0 copy-start.3
  12.8 0.0 copy-start.4
  12.8 0.0 copy-start.5
  12.8 0.0 copy-start.6
  12.8 0.0 copy-start.7
  12.8 0.0 copy-start.8
  12.9 0.0 copy-start.9
  12.9 0.0 copy-start.10
  12.9 13.3 %all_to_all.20.windows = f32[8,2,128,128]{3,2,1,0:T(8,128)S(1)} all-to-all(f32[8,2,128,128]{3,2,1,0:T(8,128)S(1)} %cut_windows.1), channel_id=1, replica_groups=mesh['tile'=64,'sec'=8] {'sec'}, dimensions={0} | all-to-all | bytes 2097152 | tf_op jit(solution)/shard_map/all_to_all | solution.py:287
  26.2 0.0 copy-done
  26.2 0.0 copy-done.2
  26.2 0.0 copy-done.3
  26.2 0.0 copy-done.4
  26.2 0.0 copy-done.5
  26.2 0.0 copy-done.6
  26.3 0.0 copy-done.7
  26.3 0.0 copy-done.8
  26.3 0.0 copy-done.9
  26.3 0.0 copy-done.10
  26.3 8.9 %wave_gradients.1 = (f32[2,128,128]{2,1,0:T(8,128)S(1)}, f32[2,128,128]{2,1,0:T(8,128)S(1)}, f32[2,8,16,128]{3,2,1,0:T(8,128)S(1)}) custom-call(s32[1]{0:T(128)} %bitcast.sec_ref, f32[8,2,128,128]{3,2,1,0:T(8,128)S(1)} %all_to_all.20.windows, f32[2,4,128,128]{3,2,1,0:T(8,128)S(1)} %copy-done, f32[2,128,128]{2,1,0:T(8,128)S(1)} %copy-done.2, ...), custom_call_target="tpu_custom_call" | custom-call | tf_op jit(solution)/shard_map/wave_gradients/pallas_call | solution.py:238
  35.2 19.6 %all_to_all.21 = f32[16,16,128]{2,1,0:T(8,128)S(1)} all-to-all(f32[16,16,128]{2,1,0:T(8,128)S(1)} %bitcast.10), channel_id=1, replica_groups={{0,8,16,24,256,264,272,280,4,12,20,28,260,268,276,284},{1,9,17,25,257,2..., dimensions={0} | all-to-all | bytes 262144 | tf_op jit(solution)/shard_map/all_to_all | solution.py:227
  54.9 0.6 broadcast_in_dim.11
  55.5 11.3 %all-to-all-start.2 = ((f32[8,16,128]{2,1,0:T(8,128)}), f32[8,16,128]{2,1,0:T(8,128)S(1)}, u32[]{:S(2)}, u32[]{:S(2)}) async-start(f32[8,16,128]{2,1,0:T(8,128)} %broadcast_in_dim.11), calls=%async_computation.2 | async-start | bytes 131072 | tf_op jit(solution)/shard_map/all_to_all | solution.py:227
  66.8 2.2 %collective-permute-start.1 = (f32[2,128,128]{2,1,0:T(8,128)S(1)}, f32[2,128,128]{2,1,0:T(8,128)S(1)}, u32[]{:S(2)}, u32[]{:S(2)}) collective-permute-start(f32[2,128,128]{2,1,0:T(8,128)S(1)} %get-tuple-element.10), channel_id=1, source_target_pairs={{0,4},{1,5},{2,6},{3,7},{4,0},{5,1},{6,2},{7,3},{8,12},{9,13},{10,... | collective-permute-start | bytes 393224 | tf_op jit(solution)/shard_map/ppermute | solution.py:293
  69.0 0.1 pad_add_fusion.sec_ref
  69.0 3.8 %collective-permute-done.1.other_grad = f32[2,128,128]{2,1,0:T(8,128)S(1)} collective-permute-done((f32[2,128,128]{2,1,0:T(8,128)S(1)}, f32[2,128,128]{2,1,0:T(8,128)S(1)}, u32[]{:S(2)}, u32[]{:S(2)}) %collective-permute-start.1) | collective-permute-done | bytes 131104 | tf_op jit(solution)/shard_map/ppermute | solution.py:293
  72.8 0.9 scatter_windows.1
  73.7 5.3 %all-to-all-done.2 = f32[8,16,128]{2,1,0:T(8,128)S(1)} async-done(((f32[8,16,128]{2,1,0:T(8,128)}), f32[8,16,128]{2,1,0:T(8,128)S(1)}, u32[]{:S(2)}, u32[]{:S(2)}) %all-to-all-start.2) | async-done | bytes 65568 | tf_op jit(solution)/shard_map/all_to_all | solution.py:227
  79.0 4.8 %collective-permute-start.2 = (f32[2,128,256]{2,1,0:T(8,128)S(1)}, f32[2,128,256]{2,1,0:T(8,128)S(1)}, u32[]{:S(2)}, u32[]{:S(2)}) collective-permute-start(f32[2,128,256]{2,1,0:T(8,128)S(1)} %get-tuple-element.15), channel_id=1, source_target_pairs={{0,8},{8,16},{16,24},{24,32},{32,40},{40,48},{48,56},{56,64},{64,7... | collective-permute-start | bytes 786440 | tf_op jit(solution)/shard_map/ppermute | solution.py:315
  83.8 9.0 %all_to_all.22 = f32[8,16,128]{2,1,0:T(8,128)S(1)} all-to-all(f32[8,16,128]{2,1,0:T(8,128)S(1)} %broadcast_in_dim.13), channel_id=1, replica_groups={{0,8,16,24,256,264,272,280},{1,9,17,25,257,265,273,281},{2,10,18,26,258..., dimensions={0} | all-to-all | bytes 131072 | tf_op jit(solution)/shard_map/all_to_all | solution.py:227
  92.8 0.0 collective-permute-done.2
  92.8 0.7 add_bitcast_fusion
  93.6 0.6 copy.18
  (3 shorter events, 0.0 us)
Async XLA Ops:
  0.6 11.2 %collective-permute-start = (f32[2,128,256]{2,1,0:T(8,128)}, f32[2,128,256]{2,1,0:T(8,128)S(1)}, u32[]{:S(2)}, u32[]{:S(2)}) collective-permute-start(f32[2,128,256]{2,1,0:T(8,128)} %bitcast.8), channel_id=1, source_target_pairs={{0,504},{8,0},{16,8},{24,16},{32,24},{40,32},{48,40},{56,48},{64,5... | collective-permute-start | bytes 786440 | tf_op jit(solution)/shard_map/ppermute | solution.py:270
  9.4 0.7 copy-start.11
  9.4 0.7 copy-start.12
  10.1 0.9 %copy-start.1 = (f32[2,1,128,256]{3,2,1,0:T(8,128)S(1)}, f32[2,1,128,256]{3,2,1,0:T(8,128)}, u32[]{:S(2)}) copy-start(f32[2,1,128,256]{3,2,1,0:T(8,128)} %param.13) | copy-start | bytes 786436
  12.8 13.5 %copy-start = (f32[2,4,128,128]{3,2,1,0:T(8,128)S(1)}, f32[2,4,128,128]{3,2,1,0:T(8,128)}, u32[]{:S(2)}) copy-start(f32[2,4,128,128]{3,2,1,0:T(8,128)} %probe.1) | copy-start | bytes 1572868
  12.8 13.4 %copy-start.2 = (f32[2,128,128]{2,1,0:T(8,128)S(1)}, f32[2,128,128]{2,1,0:T(8,128)}, u32[]{:S(2)}) copy-start(f32[2,128,128]{2,1,0:T(8,128)} %measured.1) | copy-start | bytes 393220
  12.8 13.4 %copy-start.3 = (bf16[256,256]{1,0:T(8,128)(2,1)S(1)}, bf16[256,256]{1,0:T(8,128)(2,1)}, u32[]{:S(2)}) copy-start(bf16[256,256]{1,0:T(8,128)(2,1)} %constant.24.clone.prop_high) | copy-start | bytes 393220
  12.8 13.4 %copy-start.4 = (bf16[256,256]{1,0:T(8,128)(2,1)S(1)}, bf16[256,256]{1,0:T(8,128)(2,1)}, u32[]{:S(2)}) copy-start(bf16[256,256]{1,0:T(8,128)(2,1)} %constant.25.clone.prop_low) | copy-start | bytes 393220
  12.8 13.4 %copy-start.5 = (bf16[256,256]{1,0:T(8,128)(2,1)S(1)}, bf16[256,256]{1,0:T(8,128)(2,1)}, u32[]{:S(2)}) copy-start(bf16[256,256]{1,0:T(8,128)(2,1)} %constant.26.clone.back_high) | copy-start | bytes 393220
  12.8 13.4 %copy-start.6 = (bf16[256,256]{1,0:T(8,128)(2,1)S(1)}, bf16[256,256]{1,0:T(8,128)(2,1)}, u32[]{:S(2)}) copy-start(bf16[256,256]{1,0:T(8,128)(2,1)} %constant.27.clone.back_low) | copy-start | bytes 393220
  12.8 13.4 %copy-start.7 = (bf16[256,256]{1,0:T(8,128)(2,1)S(1)}, bf16[256,256]{1,0:T(8,128)(2,1)}, u32[]{:S(2)}) copy-start(bf16[256,256]{1,0:T(8,128)(2,1)} %constant.28.clone.four_high) | copy-start | bytes 393220
  12.8 13.4 %copy-start.8 = (bf16[256,256]{1,0:T(8,128)(2,1)S(1)}, bf16[256,256]{1,0:T(8,128)(2,1)}, u32[]{:S(2)}) copy-start(bf16[256,256]{1,0:T(8,128)(2,1)} %constant.29.clone.four_low) | copy-start | bytes 393220
  12.9 13.4 %copy-start.9 = (bf16[256,256]{1,0:T(8,128)(2,1)S(1)}, bf16[256,256]{1,0:T(8,128)(2,1)}, u32[]{:S(2)}) copy-start(bf16[256,256]{1,0:T(8,128)(2,1)} %constant.30.clone.inv_high) | copy-start | bytes 393220
  12.9 13.4 %copy-start.10 = (bf16[256,256]{1,0:T(8,128)(2,1)S(1)}, bf16[256,256]{1,0:T(8,128)(2,1)}, u32[]{:S(2)}) copy-start(bf16[256,256]{1,0:T(8,128)(2,1)} %constant.31.clone.inv_low) | copy-start | bytes 393220
  55.5 23.5 %all-to-all-start.2 = ((f32[8,16,128]{2,1,0:T(8,128)}), f32[8,16,128]{2,1,0:T(8,128)S(1)}, u32[]{:S(2)}, u32[]{:S(2)}) async-start(f32[8,16,128]{2,1,0:T(8,128)} %broadcast_in_dim.11), calls=%async_computation.2 | async-start | bytes 131072 | tf_op jit(solution)/shard_map/all_to_all | solution.py:227
  66.8 6.0 %collective-permute-start.1 = (f32[2,128,128]{2,1,0:T(8,128)S(1)}, f32[2,128,128]{2,1,0:T(8,128)S(1)}, u32[]{:S(2)}, u32[]{:S(2)}) collective-permute-start(f32[2,128,128]{2,1,0:T(8,128)S(1)} %get-tuple-element.10), channel_id=1, source_target_pairs={{0,4},{1,5},{2,6},{3,7},{4,0},{5,1},{6,2},{7,3},{8,12},{9,13},{10,... | collective-permute-start | bytes 393224 | tf_op jit(solution)/shard_map/ppermute | solution.py:293
  79.0 13.8 %collective-permute-start.2 = (f32[2,128,256]{2,1,0:T(8,128)S(1)}, f32[2,128,256]{2,1,0:T(8,128)S(1)}, u32[]{:S(2)}, u32[]{:S(2)}) collective-permute-start(f32[2,128,256]{2,1,0:T(8,128)S(1)} %get-tuple-element.15), channel_id=1, source_target_pairs={{0,8},{8,16},{16,24},{24,32},{32,40},{40,48},{48,56},{56,64},{64,7... | collective-permute-start | bytes 786440 | tf_op jit(solution)/shard_map/ppermute | solution.py:315

commit v3 on v2

--- a/solution.py
+++ b/solution.py
@@ -13,6 +13,7 @@
 PHASE_RATE = 0.05
 SUBLANES = 8
 VMEM_BYTES = 48 * 1024 * 1024
+SUM_COST = 100 * 1000 * 1000
 AXES = ("tile", "sec")
 POSITION_BIT, CORE_BIT, Z_BITS, X_BIT = 2, 3, (4, 5, 6, 7), 8
 
@@ -71,7 +72,7 @@
 
 def sandwich(right, fields):
     first = [product(split(jnp.concatenate(pair, axis=1)), right) for pair in fields]
-    turned_over = [tuple(flipped(part) for part in split(half)) for half in first]
+    turned_over = [split(flipped(half)) for half in first]
     out = [product(halves, right) for halves in turned_over]
     size = fields[0][0].shape[0]
     return [(field[:, :size], field[:, size:]) for field in out]
@@ -213,6 +214,31 @@
     spill[...] = grid[:, rows:]
 
 
+def finish_kernel(owned, received, pieces, obj_grad, probe_grad):
+    obj_grad[:, 0] = owned[...] + received[...]
+    probe_grad[...] = pieces[...]
+
+
+def spread_kernel(blocks, out):
+    total = blocks[0]
+    for k in range(1, blocks.shape[0]):
+        total = total + blocks[k]
+    for k in range(out.shape[0]):
+        out[k] = total
+
+
+def summed_to(blocks, count, name):
+    return pl.pallas_call(
+        spread_kernel,
+        out_shape=jax.ShapeDtypeStruct((count,) + blocks.shape[1:], blocks.dtype),
+        in_specs=[pl.BlockSpec(memory_space=pltpu.VMEM)],
+        out_specs=pl.BlockSpec(memory_space=pltpu.VMEM),
+        compiler_params=pltpu.CompilerParams(vmem_limit_bytes=VMEM_BYTES),
+        cost_estimate=pl.CostEstimate(flops=0, bytes_accessed=SUM_COST, transcendentals=0),
+        name=name,
+    )(blocks)
+
+
 def groups_of(bits, total):
     rest = [bit for bit in range(total) if bit not in bits]
     found = []
@@ -292,10 +318,11 @@
     half = secs // 2
     other_grad = lax.ppermute(sent_grad, "sec", [(i, (i + half) % secs) for i in range(secs)])
 
-    near = (CORE_BIT, Z_BITS[0], X_BIT)
+    near, far = (CORE_BIT, Z_BITS[0], X_BIT), Z_BITS[1:]
     arrived = exchanged(bands.reshape(-1, band, size), near + (POSITION_BIT,))
-    part = jnp.sum(arrived, axis=0)
+    part = summed_to(arrived, 1 << len(far), "sum_near")
     other_grad = lax.optimization_barrier((other_grad, part))[0]
+    arrived = exchanged(part, far)
 
     owned, spill = pl.pallas_call(
         scatter_kernel,
@@ -309,15 +336,20 @@
         compiler_params=params,
         name="scatter_windows",
     )(jnp.stack([sec, jnp.int32(secs)]), row_offset, col_offset, own_grad, other_grad)
-    far_bits = Z_BITS[1:]
-    part = jnp.sum(exchanged(jnp.broadcast_to(part, (1 << len(far_bits),) + part.shape), far_bits), axis=0)
-    spill = lax.optimization_barrier((spill, part))[0]
     received = lax.ppermute(spill, "tile", [(i, (i + 1) % tiles) for i in range(tiles)])
 
-    pieces = exchanged(jnp.broadcast_to(part, (1 << len(near),) + part.shape), near)
-    obj_grad = (owned + received)[:, None]
-    probe_grad = pieces.reshape(2, modes, band, size)
-    return (obj_grad, probe_grad)
+    pieces = exchanged(summed_to(arrived, 1 << len(near), "sum_far"), near)
+    return pl.pallas_call(
+        finish_kernel,
+        out_shape=(
+            jax.ShapeDtypeStruct((2, 1, rows, cols), f32),
+            jax.ShapeDtypeStruct((2, modes, band, size), f32),
+        ),
+        in_specs=[vmem, vmem, vmem],
+        out_specs=(vmem, vmem),
+        compiler_params=params,
+        name="finish",
+    )(owned, received, pieces.reshape(2, modes, band, size))
 
 
 def solution(mesh):

time: 94.6 us -> 91.7 us (0.969)
  blocking collectives: 41.9 us -> 32.9 us
  starting transfers between devices: 27 us -> 31.8 us
  Pallas kernels: 11.5 us -> 13.2 us
  waiting for transfers between devices: 9.07 us -> 10.7 us
  local copies, waits for them, and re-layouts: 2.94 us -> 1.67 us
    all_to_all x2 -> x1, blocking collectives: 28.6 us -> 19.6 us  [exchanged(): lax.all_to_all(blocks, AXES, 0, 0, axis_index_groups=groups_of(bits, total))]
    all_to_all x1 -> x2, starting transfers between devices: 11.3 us -> 16.8 us  [exchanged(): lax.all_to_all(blocks, AXES, 0, 0, axis_index_groups=groups_of(bits, total))]
    pallas_call x0 -> x3, Pallas kernels: none -> 2.04 us  [the longest x2 1.29 us: summed_to(): pl.pallas_call(spread_kernel, out_shape=jax.ShapeDtypeStruct((count,) + b...]
    all_to_all x1 -> x2, waiting for transfers between devices: 5.29 us -> 6.97 us  [exchanged(): lax.all_to_all(blocks, AXES, 0, 0, axis_index_groups=groups_of(bits, total))]
    unnamed x27 -> x26, local copies, waits for them, and re-layouts: 2.3 us -> 1.67 us
  transfers between devices with their start and end apart: 4 -> 5, of which waited for: 2 -> 3; matrix products, arithmetic and copies ran while one was open for 0% -> 0% of each run, Pallas kernels for 2% -> 2%
where the time goes in v3:
time: 91.7 us; the launch traced here: 91.2 us
  blocking collectives  32.9 us (36%)
  starting transfers between devices  31.8 us (35%)
  Pallas kernels  13.2 us (14%)
  waiting for transfers between devices  10.7 us (12%)
  local copies, waits for them, and re-layouts  1.67 us (2%)
    all_to_all x1, blocking collectives, exchanged(): lax.all_to_all(blocks, AXES, 0, 0, axis_index_groups=groups_of(bits, total))  19.6 us
    all_to_all x2, starting transfers between devices, exchanged(): lax.all_to_all(blocks, AXES, 0, 0, axis_index_groups=groups_of(bits, total))  16.8 us
    all_to_all x1, blocking collectives, per_device(): windows = lax.all_to_all(cut, 'sec', 0, 0)  13.3 us
    ppermute x1, starting transfers between devices, per_device(): lax.ppermute(own, 'tile', [(i, (i - 1) % tiles) for i in range(tiles)])  8.79 us
    pallas_call x1, Pallas kernels, wave_call(): pl.pallas_call(functools.partial(wave_kernel, 1.0 / positions), out_shape...  8.57 us
    all_to_all x2, waiting for transfers between devices, exchanged(): lax.all_to_all(blocks, AXES, 0, 0, axis_index_groups=groups_of(bits, total))  6.97 us
    ppermute x1, starting transfers between devices, per_device(): lax.ppermute(spill, 'tile', [(i, (i + 1) % tiles) for i in range(tiles)])  4.01 us
    ppermute x1, waiting for transfers between devices, per_device(): lax.ppermute(sent_grad, 'sec', [(i, (i + half) % secs) for i in range(sec...  3.77 us
  transfers between devices with their start and end apart: 5, of which 3 were waited for; matrix products, arithmetic and copies ran while one was open for 0% of the time, Pallas kernels for 2%

profile of v3, /device:TPU:1, one launch (start us, length us, event | category | flops | bytes accessed | tf_op | source)
XLA Modules:
  0.0 91.2 jit_solution(9359195940022329442)
XLA Ops:
  0.6 8.8 %collective-permute-start = (f32[2,128,256]{2,1,0:T(8,128)}, f32[2,128,256]{2,1,0:T(8,128)S(1)}, u32[]{:S(2)}, u32[]{:S(2)}) collective-permute-start(f32[2,128,256]{2,1,0:T(8,128)} %bitcast.5), channel_id=1, source_target_pairs={{0,504},{8,0},{16,8},{24,16},{32,24},{40,32},{48,40},{56,48},{64,5... | collective-permute-start | bytes 786440 | tf_op jit(solution)/shard_map/ppermute | solution.py:296
  9.4 0.0 copy-start.11
  9.4 0.0 copy-start.12
  9.4 0.6 copy-done.11
  10.1 0.0 copy-done.12
  10.1 0.0 copy-start.1
  10.1 0.9 %copy-done.1 = f32[2,1,128,256]{3,2,1,0:T(8,128)S(1)} copy-done((f32[2,1,128,256]{3,2,1,0:T(8,128)S(1)}, f32[2,1,128,256]{3,2,1,0:T(8,128)}, u32[]{:S(2)}) %copy-start.1) | copy-done | bytes 262168
  11.1 0.8 own_windows.1.own
  11.8 0.0 collective-permute-done.rim
  11.8 0.9 %cut_windows.1 = f32[8,2,128,128]{3,2,1,0:T(8,128)S(1)} custom-call(s32[1]{0:T(128)} %bitcast.sec_ref, s32[2]{0:T(128)S(1)} %copy-done.11, s32[2]{0:T(128)S(1)} %copy-done.12, f32[2,2,128,128]{3,2,1,0:T(8,128)S(1)} %own_windows.1.own, f32[2,128,256]{2,1,0:T(8,128)S(1)} %collective-permute-done.rim), custom_call_target="tpu_custom_call" | custom-call | tf_op jit(solution)/shard_map/cut_windows/pallas_call | solution.py:305
  12.8 0.0 copy-start
  12.8 0.0 copy-start.2
  12.8 0.0 copy-start.3
  12.8 0.0 copy-start.4
  12.8 0.0 copy-start.5
  12.8 0.0 copy-start.6
  12.8 0.0 copy-start.7
  12.8 0.0 copy-start.8
  12.9 0.0 copy-start.9
  12.9 0.0 copy-start.10
  12.9 13.3 %all_to_all.20.windows = f32[8,2,128,128]{3,2,1,0:T(8,128)S(1)} all-to-all(f32[8,2,128,128]{3,2,1,0:T(8,128)S(1)} %cut_windows.1), channel_id=1, replica_groups=mesh['tile'=64,'sec'=8] {'sec'}, dimensions={0} | all-to-all | bytes 2097152 | tf_op jit(solution)/shard_map/all_to_all | solution.py:313
  26.2 0.0 copy-done
  26.2 0.0 copy-done.2
  26.2 0.0 copy-done.3
  26.2 0.0 copy-done.4
  26.2 0.0 copy-done.5
  26.2 0.0 copy-done.6
  26.3 0.0 copy-done.7
  26.3 0.0 copy-done.8
  26.3 0.0 copy-done.9
  26.3 0.0 copy-done.10
  26.3 8.6 %wave_gradients.1 = (f32[2,128,128]{2,1,0:T(8,128)S(1)}, f32[2,128,128]{2,1,0:T(8,128)S(1)}, f32[2,8,16,128]{3,2,1,0:T(8,128)S(1)}) custom-call(s32[1]{0:T(128)} %bitcast.sec_ref, f32[8,2,128,128]{3,2,1,0:T(8,128)S(1)} %all_to_all.20.windows, f32[2,4,128,128]{3,2,1,0:T(8,128)S(1)} %copy-done, f32[2,128,128]{2,1,0:T(8,128)S(1)} %copy-done.2, ...), custom_call_target="tpu_custom_call" | custom-call | tf_op jit(solution)/shard_map/wave_gradients/pallas_call | solution.py:264
  34.9 19.6 %all_to_all.21.blocks = f32[16,16,128]{2,1,0:T(8,128)S(1)} all-to-all(f32[16,16,128]{2,1,0:T(8,128)S(1)} %bitcast.7), channel_id=1, replica_groups={{0,8,16,24,256,264,272,280,4,12,20,28,260,268,276,284},{1,9,17,25,257,2..., dimensions={0} | all-to-all | bytes 262144 | tf_op jit(solution)/shard_map/all_to_all | solution.py:253
  54.5 0.6 sum_near.1
  55.1 11.3 %all-to-all-start.2 = ((f32[8,16,128]{2,1,0:T(8,128)}), f32[8,16,128]{2,1,0:T(8,128)S(1)}, u32[]{:S(2)}, u32[]{:S(2)}) async-start(f32[8,16,128]{2,1,0:T(8,128)} %sum_near.1), calls=%async_computation.2 | async-start | bytes 131072 | tf_op jit(solution)/shard_map/all_to_all | solution.py:253
  66.4 2.2 %collective-permute-start.1 = (f32[2,128,128]{2,1,0:T(8,128)S(1)}, f32[2,128,128]{2,1,0:T(8,128)S(1)}, u32[]{:S(2)}, u32[]{:S(2)}) collective-permute-start(f32[2,128,128]{2,1,0:T(8,128)S(1)} %get-tuple-element.9), channel_id=1, source_target_pairs={{0,4},{1,5},{2,6},{3,7},{4,0},{5,1},{6,2},{7,3},{8,12},{9,13},{10,... | collective-permute-start | bytes 393224 | tf_op jit(solution)/shard_map/ppermute | solution.py:319
  68.6 0.1 pad_add_fusion.sec_ref
  68.7 3.8 %collective-permute-done.1.other_grad = f32[2,128,128]{2,1,0:T(8,128)S(1)} collective-permute-done((f32[2,128,128]{2,1,0:T(8,128)S(1)}, f32[2,128,128]{2,1,0:T(8,128)S(1)}, u32[]{:S(2)}, u32[]{:S(2)}) %collective-permute-start.1) | collective-permute-done | bytes 131104 | tf_op jit(solution)/shard_map/ppermute | solution.py:319
  72.4 0.9 scatter_windows.1
  73.3 4.0 %collective-permute-start.2 = (f32[2,128,256]{2,1,0:T(8,128)S(1)}, f32[2,128,256]{2,1,0:T(8,128)S(1)}, u32[]{:S(2)}, u32[]{:S(2)}) collective-permute-start(f32[2,128,256]{2,1,0:T(8,128)S(1)} %get-tuple-element.13), channel_id=1, source_target_pairs={{0,8},{8,16},{16,24},{24,32},{32,40},{40,48},{48,56},{56,64},{64,7... | collective-permute-start | bytes 786440 | tf_op jit(solution)/shard_map/ppermute | solution.py:339
  77.4 1.3 %all-to-all-done.2.blocks = f32[8,16,128]{2,1,0:T(8,128)S(1)} async-done(((f32[8,16,128]{2,1,0:T(8,128)}), f32[8,16,128]{2,1,0:T(8,128)S(1)}, u32[]{:S(2)}, u32[]{:S(2)}) %all-to-all-start.2) | async-done | bytes 65568 | tf_op jit(solution)/shard_map/all_to_all | solution.py:253
  78.6 0.6 sum_far.1
  79.3 5.5 %all-to-all-start.3 = ((f32[8,16,128]{2,1,0:T(8,128)}), f32[8,16,128]{2,1,0:T(8,128)S(1)}, u32[]{:S(2)}, u32[]{:S(2)}) async-start(f32[8,16,128]{2,1,0:T(8,128)} %sum_far.1), calls=%async_computation.3 | async-start | bytes 131072 | tf_op jit(solution)/shard_map/all_to_all | solution.py:253
  84.8 0.0 collective-permute-done.2.received
  84.8 5.7 %all-to-all-done.3 = f32[8,16,128]{2,1,0:T(8,128)S(1)} async-done(((f32[8,16,128]{2,1,0:T(8,128)}), f32[8,16,128]{2,1,0:T(8,128)S(1)}, u32[]{:S(2)}, u32[]{:S(2)}) %all-to-all-start.3) | async-done | bytes 65568 | tf_op jit(solution)/shard_map/all_to_all | solution.py:253
  90.5 0.7 finish.1
Async XLA Ops:
  0.6 11.2 %collective-permute-start = (f32[2,128,256]{2,1,0:T(8,128)}, f32[2,128,256]{2,1,0:T(8,128)S(1)}, u32[]{:S(2)}, u32[]{:S(2)}) collective-permute-start(f32[2,128,256]{2,1,0:T(8,128)} %bitcast.5), channel_id=1, source_target_pairs={{0,504},{8,0},{16,8},{24,16},{32,24},{40,32},{48,40},{56,48},{64,5... | collective-permute-start | bytes 786440 | tf_op jit(solution)/shard_map/ppermute | solution.py:296
  9.4 0.7 copy-start.11
  9.4 0.7 copy-start.12
  10.1 0.9 %copy-start.1 = (f32[2,1,128,256]{3,2,1,0:T(8,128)S(1)}, f32[2,1,128,256]{3,2,1,0:T(8,128)}, u32[]{:S(2)}) copy-start(f32[2,1,128,256]{3,2,1,0:T(8,128)} %param.13) | copy-start | bytes 786436
  12.8 13.5 %copy-start = (f32[2,4,128,128]{3,2,1,0:T(8,128)S(1)}, f32[2,4,128,128]{3,2,1,0:T(8,128)}, u32[]{:S(2)}) copy-start(f32[2,4,128,128]{3,2,1,0:T(8,128)} %probe.1) | copy-start | bytes 1572868
  12.8 13.4 %copy-start.2 = (f32[2,128,128]{2,1,0:T(8,128)S(1)}, f32[2,128,128]{2,1,0:T(8,128)}, u32[]{:S(2)}) copy-start(f32[2,128,128]{2,1,0:T(8,128)} %measured.1) | copy-start | bytes 393220
  12.8 13.4 %copy-start.3 = (bf16[256,256]{1,0:T(8,128)(2,1)S(1)}, bf16[256,256]{1,0:T(8,128)(2,1)}, u32[]{:S(2)}) copy-start(bf16[256,256]{1,0:T(8,128)(2,1)} %constant.22.clone.prop_high) | copy-start | bytes 393220
  12.8 13.4 %copy-start.4 = (bf16[256,256]{1,0:T(8,128)(2,1)S(1)}, bf16[256,256]{1,0:T(8,128)(2,1)}, u32[]{:S(2)}) copy-start(bf16[256,256]{1,0:T(8,128)(2,1)} %constant.23.clone.prop_low) | copy-start | bytes 393220
  12.8 13.4 %copy-start.5 = (bf16[256,256]{1,0:T(8,128)(2,1)S(1)}, bf16[256,256]{1,0:T(8,128)(2,1)}, u32[]{:S(2)}) copy-start(bf16[256,256]{1,0:T(8,128)(2,1)} %constant.24.clone.back_high) | copy-start | bytes 393220
  12.8 13.4 %copy-start.6 = (bf16[256,256]{1,0:T(8,128)(2,1)S(1)}, bf16[256,256]{1,0:T(8,128)(2,1)}, u32[]{:S(2)}) copy-start(bf16[256,256]{1,0:T(8,128)(2,1)} %constant.25.clone.back_low) | copy-start | bytes 393220
  12.8 13.4 %copy-start.7 = (bf16[256,256]{1,0:T(8,128)(2,1)S(1)}, bf16[256,256]{1,0:T(8,128)(2,1)}, u32[]{:S(2)}) copy-start(bf16[256,256]{1,0:T(8,128)(2,1)} %constant.26.clone.four_high) | copy-start | bytes 393220
  12.8 13.4 %copy-start.8 = (bf16[256,256]{1,0:T(8,128)(2,1)S(1)}, bf16[256,256]{1,0:T(8,128)(2,1)}, u32[]{:S(2)}) copy-start(bf16[256,256]{1,0:T(8,128)(2,1)} %constant.27.clone.four_low) | copy-start | bytes 393220
  12.9 13.4 %copy-start.9 = (bf16[256,256]{1,0:T(8,128)(2,1)S(1)}, bf16[256,256]{1,0:T(8,128)(2,1)}, u32[]{:S(2)}) copy-start(bf16[256,256]{1,0:T(8,128)(2,1)} %constant.28.clone.inv_high) | copy-start | bytes 393220
  12.9 13.4 %copy-start.10 = (bf16[256,256]{1,0:T(8,128)(2,1)S(1)}, bf16[256,256]{1,0:T(8,128)(2,1)}, u32[]{:S(2)}) copy-start(bf16[256,256]{1,0:T(8,128)(2,1)} %constant.29.clone.inv_low) | copy-start | bytes 393220
  55.1 23.5 %all-to-all-start.2 = ((f32[8,16,128]{2,1,0:T(8,128)}), f32[8,16,128]{2,1,0:T(8,128)S(1)}, u32[]{:S(2)}, u32[]{:S(2)}) async-start(f32[8,16,128]{2,1,0:T(8,128)} %sum_near.1), calls=%async_computation.2 | async-start | bytes 131072 | tf_op jit(solution)/shard_map/all_to_all | solution.py:253
  66.4 6.0 %collective-permute-start.1 = (f32[2,128,128]{2,1,0:T(8,128)S(1)}, f32[2,128,128]{2,1,0:T(8,128)S(1)}, u32[]{:S(2)}, u32[]{:S(2)}) collective-permute-start(f32[2,128,128]{2,1,0:T(8,128)S(1)} %get-tuple-element.9), channel_id=1, source_target_pairs={{0,4},{1,5},{2,6},{3,7},{4,0},{5,1},{6,2},{7,3},{8,12},{9,13},{10,... | collective-permute-start | bytes 393224 | tf_op jit(solution)/shard_map/ppermute | solution.py:319
  73.3 11.4 %collective-permute-start.2 = (f32[2,128,256]{2,1,0:T(8,128)S(1)}, f32[2,128,256]{2,1,0:T(8,128)S(1)}, u32[]{:S(2)}, u32[]{:S(2)}) collective-permute-start(f32[2,128,256]{2,1,0:T(8,128)S(1)} %get-tuple-element.13), channel_id=1, source_target_pairs={{0,8},{8,16},{16,24},{24,32},{32,40},{40,48},{48,56},{56,64},{64,7... | collective-permute-start | bytes 786440 | tf_op jit(solution)/shard_map/ppermute | solution.py:339
  79.3 11.2 %all-to-all-start.3 = ((f32[8,16,128]{2,1,0:T(8,128)}), f32[8,16,128]{2,1,0:T(8,128)S(1)}, u32[]{:S(2)}, u32[]{:S(2)}) async-start(f32[8,16,128]{2,1,0:T(8,128)} %sum_far.1), calls=%async_computation.3 | async-start | bytes 131072 | tf_op jit(solution)/shard_map/all_to_all | solution.py:253

commit v4 on v3

--- a/solution.py
+++ b/solution.py
@@ -11,6 +11,7 @@
 from jax.sharding import PartitionSpec as P
 
 PHASE_RATE = 0.05
+ORDER = (0, 6, 3, 5, 1, 7, 2, 4)
 SUBLANES = 8
 VMEM_BYTES = 48 * 1024 * 1024
 SUM_COST = 100 * 1000 * 1000
@@ -67,7 +68,8 @@
 
 def product(halves, right):
     high, low = halves
-    return dot(high, right[0][...]) + (dot(low, right[0][...]) + dot(high, right[1][...]))
+    tall = dot(jnp.concatenate([high, low], axis=0), right[0][...])
+    return tall[: high.shape[0]] + (tall[high.shape[0] :] + dot(high, right[1][...]))
 
 
 def sandwich(right, fields):
@@ -110,7 +112,7 @@
     waves[0] = probe[...]
 
     def exits(step):
-        win_re, win_im = windows[step, 0], windows[step, 1]
+        win_re, win_im = windows[ORDER.index(step), 0], windows[ORDER.index(step), 1]
         found = []
         for k in range(modes):
             wave_re, wave_im = waves[step, 0, k], waves[step, 1, k]
@@ -139,7 +141,7 @@
         window_grads[step, 1] = total_im.T if step % 2 else total_im
 
     def entering(step):
-        win_re, win_im = windows[step, 0], windows[step, 1]
+        win_re, win_im = windows[ORDER.index(step), 0], windows[ORDER.index(step), 1]
         found = []
         for k in range(modes):
             grad_re, grad_im = grads[0, k], grads[1, k]
@@ -194,7 +196,7 @@
             window = jnp.where(place < size - row, own[position, part], beyond)
             window = jnp.where(odd, window.T, window)
             for sec in range(position * secs // count, (position + 1) * secs // count):
-                cut[sec, part] = window
+                cut[ORDER.index(sec), part] = window
 
 
 def scatter_kernel(sec_ref, row_ref, col_ref, own_grad, other_grad, owned, spill, grid):
@@ -310,7 +312,8 @@
         compiler_params=params,
         name="cut_windows",
     )(sec[None], row_offset, col_offset, own_windows, rim)
-    windows = lax.all_to_all(cut, "sec", 0, 0)
+    ranks = [[tile * secs + place for place in ORDER] for tile in range(tiles)]
+    windows = lax.all_to_all(cut, AXES, 0, 0, axis_index_groups=ranks)
 
     own_grad, sent_grad, bands = wave_call(sec[None], windows, probe, measured, measured.shape[0] * tiles)
 
@@ -318,7 +321,7 @@
     half = secs // 2
     other_grad = lax.ppermute(sent_grad, "sec", [(i, (i + half) % secs) for i in range(secs)])
 
-    near, far = (CORE_BIT, Z_BITS[0], X_BIT), Z_BITS[1:]
+    near, far = (CORE_BIT, Z_BITS[0], X_BIT), Z_BITS[:0:-1]
     arrived = exchanged(bands.reshape(-1, band, size), near + (POSITION_BIT,))
     part = summed_to(arrived, 1 << len(far), "sum_near")
     other_grad = lax.optimization_barrier((other_grad, part))[0]

time: 91.7 us -> 90.4 us (0.986)
  transfers between devices with their start and end apart: 5 -> 5, of which waited for: 3 -> 3; matrix products, arithmetic and copies ran while one was open for 0% -> 0% of each run, Pallas kernels for 2% -> 3%
where the time goes in v4:
time: 90.4 us; the launch traced here: 89.9 us
  blocking collectives  32.6 us (36%)
  starting transfers between devices  31.7 us (35%)
  Pallas kernels  13.1 us (14%)
  waiting for transfers between devices  9.95 us (11%)
  local copies, waits for them, and re-layouts  1.67 us (2%)
    all_to_all x1, blocking collectives, exchanged(): lax.all_to_all(blocks, AXES, 0, 0, axis_index_groups=groups_of(bits, total))  19.6 us
    all_to_all x2, starting transfers between devices, exchanged(): lax.all_to_all(blocks, AXES, 0, 0, axis_index_groups=groups_of(bits, total))  16.7 us
    all_to_all x1, blocking collectives, per_device(): windows = lax.all_to_all(cut, AXES, 0, 0, axis_index_groups=ranks)  13 us
    ppermute x1, starting transfers between devices, per_device(): lax.ppermute(own, 'tile', [(i, (i - 1) % tiles) for i in range(tiles)])  8.79 us
    pallas_call x1, Pallas kernels, wave_call(): pl.pallas_call(functools.partial(wave_kernel, 1.0 / positions), out_shape...  8.46 us
    all_to_all x2, waiting for transfers between devices, exchanged(): lax.all_to_all(blocks, AXES, 0, 0, axis_index_groups=groups_of(bits, total))  6.17 us
    ppermute x1, starting transfers between devices, per_device(): lax.ppermute(spill, 'tile', [(i, (i + 1) % tiles) for i in range(tiles)])  4.01 us
    ppermute x1, waiting for transfers between devices, per_device(): lax.ppermute(sent_grad, 'sec', [(i, (i + half) % secs) for i in range(sec...  3.77 us
  transfers between devices with their start and end apart: 5, of which 3 were waited for; matrix products, arithmetic and copies ran while one was open for 0% of the time, Pallas kernels for 3%

profile of v4, /device:TPU:1, one launch (start us, length us, event | category | flops | bytes accessed | tf_op | source)
XLA Modules:
  0.0 89.9 jit_solution(8785841446307610827)
XLA Ops:
  0.6 8.8 %collective-permute-start = (f32[2,128,256]{2,1,0:T(8,128)}, f32[2,128,256]{2,1,0:T(8,128)S(1)}, u32[]{:S(2)}, u32[]{:S(2)}) collective-permute-start(f32[2,128,256]{2,1,0:T(8,128)} %bitcast.5), channel_id=1, source_target_pairs={{0,504},{8,0},{16,8},{24,16},{32,24},{40,32},{48,40},{56,48},{64,5... | collective-permute-start | bytes 786440 | tf_op jit(solution)/shard_map/ppermute | solution.py:298
  9.4 0.0 copy-start.11
  9.4 0.0 copy-start.12
  9.4 0.6 copy-done.11
  10.1 0.0 copy-done.12
  10.1 0.0 copy-start.1
  10.1 0.9 %copy-done.1 = f32[2,1,128,256]{3,2,1,0:T(8,128)S(1)} copy-done((f32[2,1,128,256]{3,2,1,0:T(8,128)S(1)}, f32[2,1,128,256]{3,2,1,0:T(8,128)}, u32[]{:S(2)}) %copy-start.1) | copy-done | bytes 262168
  11.1 0.8 own_windows.1.own
  11.8 0.0 collective-permute-done.rim
  11.8 0.9 %cut_windows.1 = f32[8,2,128,128]{3,2,1,0:T(8,128)S(1)} custom-call(s32[1]{0:T(128)} %bitcast.sec_ref, s32[2]{0:T(128)S(1)} %copy-done.11, s32[2]{0:T(128)S(1)} %copy-done.12, f32[2,2,128,128]{3,2,1,0:T(8,128)S(1)} %own_windows.1.own, f32[2,128,256]{2,1,0:T(8,128)S(1)} %collective-permute-done.rim), custom_call_target="tpu_custom_call" | custom-call | tf_op jit(solution)/shard_map/cut_windows/pallas_call | solution.py:307
  12.8 0.0 copy-start
  12.8 0.0 copy-start.2
  12.8 0.0 copy-start.3
  12.8 0.0 copy-start.4
  12.8 0.0 copy-start.5
  12.8 0.0 copy-start.6
  12.8 0.0 copy-start.7
  12.8 0.0 copy-start.8
  12.9 0.0 copy-start.9
  12.9 0.0 copy-start.10
  12.9 13.0 %all_to_all.20.windows = f32[8,2,128,128]{3,2,1,0:T(8,128)S(1)} all-to-all(f32[8,2,128,128]{3,2,1,0:T(8,128)S(1)} %cut_windows.1), channel_id=1, replica_groups={{0,6,3,5,1,7,2,4},{8,14,11,13,9,15,10,12},{16,22,19,21,17,23,18,20},{24..., dimensions={0} | all-to-all | bytes 2097152 | tf_op jit(solution)/shard_map/all_to_all | solution.py:316
  25.9 0.0 copy-done
  25.9 0.0 copy-done.2
  25.9 0.0 copy-done.3
  25.9 0.0 copy-done.4
  25.9 0.0 copy-done.5
  25.9 0.0 copy-done.6
  25.9 0.0 copy-done.7
  25.9 0.0 copy-done.8
  25.9 0.0 copy-done.9
  25.9 0.0 copy-done.10
  25.9 8.5 %wave_gradients.1 = (f32[2,128,128]{2,1,0:T(8,128)S(1)}, f32[2,128,128]{2,1,0:T(8,128)S(1)}, f32[2,8,16,128]{3,2,1,0:T(8,128)S(1)}) custom-call(s32[1]{0:T(128)} %bitcast.sec_ref, f32[8,2,128,128]{3,2,1,0:T(8,128)S(1)} %all_to_all.20.windows, f32[2,4,128,128]{3,2,1,0:T(8,128)S(1)} %copy-done, f32[2,128,128]{2,1,0:T(8,128)S(1)} %copy-done.2, ...), custom_call_target="tpu_custom_call" | custom-call | tf_op jit(solution)/shard_map/wave_gradients/pallas_call | solution.py:266
  34.4 19.6 %all_to_all.21.blocks = f32[16,16,128]{2,1,0:T(8,128)S(1)} all-to-all(f32[16,16,128]{2,1,0:T(8,128)S(1)} %bitcast.7), channel_id=1, replica_groups={{0,8,16,24,256,264,272,280,4,12,20,28,260,268,276,284},{1,9,17,25,257,2..., dimensions={0} | all-to-all | bytes 262144 | tf_op jit(solution)/shard_map/all_to_all | solution.py:255
  54.0 0.6 sum_near.1
  54.7 11.4 %all-to-all-start.2 = ((f32[8,16,128]{2,1,0:T(8,128)}), f32[8,16,128]{2,1,0:T(8,128)S(1)}, u32[]{:S(2)}, u32[]{:S(2)}) async-start(f32[8,16,128]{2,1,0:T(8,128)} %sum_near.1), calls=%async_computation.2 | async-start | bytes 131072 | tf_op jit(solution)/shard_map/all_to_all | solution.py:255
  66.1 2.2 %collective-permute-start.1 = (f32[2,128,128]{2,1,0:T(8,128)S(1)}, f32[2,128,128]{2,1,0:T(8,128)S(1)}, u32[]{:S(2)}, u32[]{:S(2)}) collective-permute-start(f32[2,128,128]{2,1,0:T(8,128)S(1)} %get-tuple-element.9), channel_id=1, source_target_pairs={{0,4},{1,5},{2,6},{3,7},{4,0},{5,1},{6,2},{7,3},{8,12},{9,13},{10,... | collective-permute-start | bytes 393224 | tf_op jit(solution)/shard_map/ppermute | solution.py:322
  68.3 0.1 pad_add_fusion.sec_ref
  68.4 3.8 %collective-permute-done.1.other_grad = f32[2,128,128]{2,1,0:T(8,128)S(1)} collective-permute-done((f32[2,128,128]{2,1,0:T(8,128)S(1)}, f32[2,128,128]{2,1,0:T(8,128)S(1)}, u32[]{:S(2)}, u32[]{:S(2)}) %collective-permute-start.1) | collective-permute-done | bytes 131104 | tf_op jit(solution)/shard_map/ppermute | solution.py:322
  72.2 0.9 scatter_windows.1
  73.1 4.0 %collective-permute-start.2 = (f32[2,128,256]{2,1,0:T(8,128)S(1)}, f32[2,128,256]{2,1,0:T(8,128)S(1)}, u32[]{:S(2)}, u32[]{:S(2)}) collective-permute-start(f32[2,128,256]{2,1,0:T(8,128)S(1)} %get-tuple-element.13), channel_id=1, source_target_pairs={{0,8},{8,16},{16,24},{24,32},{32,40},{40,48},{48,56},{56,64},{64,7... | collective-permute-start | bytes 786440 | tf_op jit(solution)/shard_map/ppermute | solution.py:342
  77.1 0.5 all-to-all-done.2.blocks
  77.6 0.6 sum_far.1
  78.2 5.3 %all-to-all-start.3 = ((f32[8,16,128]{2,1,0:T(8,128)}), f32[8,16,128]{2,1,0:T(8,128)S(1)}, u32[]{:S(2)}, u32[]{:S(2)}) async-start(f32[8,16,128]{2,1,0:T(8,128)} %sum_far.1), calls=%async_computation.3 | async-start | bytes 131072 | tf_op jit(solution)/shard_map/all_to_all | solution.py:255
  83.5 0.0 collective-permute-done.2.received
  83.5 5.7 %all-to-all-done.3 = f32[8,16,128]{2,1,0:T(8,128)S(1)} async-done(((f32[8,16,128]{2,1,0:T(8,128)}), f32[8,16,128]{2,1,0:T(8,128)S(1)}, u32[]{:S(2)}, u32[]{:S(2)}) %all-to-all-start.3) | async-done | bytes 65568 | tf_op jit(solution)/shard_map/all_to_all | solution.py:255
  89.2 0.7 finish.1
Async XLA Ops:
  0.6 11.2 %collective-permute-start = (f32[2,128,256]{2,1,0:T(8,128)}, f32[2,128,256]{2,1,0:T(8,128)S(1)}, u32[]{:S(2)}, u32[]{:S(2)}) collective-permute-start(f32[2,128,256]{2,1,0:T(8,128)} %bitcast.5), channel_id=1, source_target_pairs={{0,504},{8,0},{16,8},{24,16},{32,24},{40,32},{48,40},{56,48},{64,5... | collective-permute-start | bytes 786440 | tf_op jit(solution)/shard_map/ppermute | solution.py:298
  9.4 0.7 copy-start.11
  9.4 0.7 copy-start.12
  10.1 0.9 %copy-start.1 = (f32[2,1,128,256]{3,2,1,0:T(8,128)S(1)}, f32[2,1,128,256]{3,2,1,0:T(8,128)}, u32[]{:S(2)}) copy-start(f32[2,1,128,256]{3,2,1,0:T(8,128)} %param.13) | copy-start | bytes 786436
  12.8 13.1 %copy-start = (f32[2,4,128,128]{3,2,1,0:T(8,128)S(1)}, f32[2,4,128,128]{3,2,1,0:T(8,128)}, u32[]{:S(2)}) copy-start(f32[2,4,128,128]{3,2,1,0:T(8,128)} %probe.1) | copy-start | bytes 1572868
  12.8 13.1 %copy-start.2 = (f32[2,128,128]{2,1,0:T(8,128)S(1)}, f32[2,128,128]{2,1,0:T(8,128)}, u32[]{:S(2)}) copy-start(f32[2,128,128]{2,1,0:T(8,128)} %measured.1) | copy-start | bytes 393220
  12.8 13.1 %copy-start.3 = (bf16[256,256]{1,0:T(8,128)(2,1)S(1)}, bf16[256,256]{1,0:T(8,128)(2,1)}, u32[]{:S(2)}) copy-start(bf16[256,256]{1,0:T(8,128)(2,1)} %constant.22.clone.prop_high) | copy-start | bytes 393220
  12.8 13.1 %copy-start.4 = (bf16[256,256]{1,0:T(8,128)(2,1)S(1)}, bf16[256,256]{1,0:T(8,128)(2,1)}, u32[]{:S(2)}) copy-start(bf16[256,256]{1,0:T(8,128)(2,1)} %constant.23.clone.prop_low) | copy-start | bytes 393220
  12.8 13.1 %copy-start.5 = (bf16[256,256]{1,0:T(8,128)(2,1)S(1)}, bf16[256,256]{1,0:T(8,128)(2,1)}, u32[]{:S(2)}) copy-start(bf16[256,256]{1,0:T(8,128)(2,1)} %constant.24.clone.back_high) | copy-start | bytes 393220
  12.8 13.1 %copy-start.6 = (bf16[256,256]{1,0:T(8,128)(2,1)S(1)}, bf16[256,256]{1,0:T(8,128)(2,1)}, u32[]{:S(2)}) copy-start(bf16[256,256]{1,0:T(8,128)(2,1)} %constant.25.clone.back_low) | copy-start | bytes 393220
  12.8 13.1 %copy-start.7 = (bf16[256,256]{1,0:T(8,128)(2,1)S(1)}, bf16[256,256]{1,0:T(8,128)(2,1)}, u32[]{:S(2)}) copy-start(bf16[256,256]{1,0:T(8,128)(2,1)} %constant.26.clone.four_high) | copy-start | bytes 393220
  12.8 13.1 %copy-start.8 = (bf16[256,256]{1,0:T(8,128)(2,1)S(1)}, bf16[256,256]{1,0:T(8,128)(2,1)}, u32[]{:S(2)}) copy-start(bf16[256,256]{1,0:T(8,128)(2,1)} %constant.27.clone.four_low) | copy-start | bytes 393220
  12.9 13.1 %copy-start.9 = (bf16[256,256]{1,0:T(8,128)(2,1)S(1)}, bf16[256,256]{1,0:T(8,128)(2,1)}, u32[]{:S(2)}) copy-start(bf16[256,256]{1,0:T(8,128)(2,1)} %constant.28.clone.inv_high) | copy-start | bytes 393220
  12.9 13.1 %copy-start.10 = (bf16[256,256]{1,0:T(8,128)(2,1)S(1)}, bf16[256,256]{1,0:T(8,128)(2,1)}, u32[]{:S(2)}) copy-start(bf16[256,256]{1,0:T(8,128)(2,1)} %constant.29.clone.inv_low) | copy-start | bytes 393220
  54.7 22.9 %all-to-all-start.2 = ((f32[8,16,128]{2,1,0:T(8,128)}), f32[8,16,128]{2,1,0:T(8,128)S(1)}, u32[]{:S(2)}, u32[]{:S(2)}) async-start(f32[8,16,128]{2,1,0:T(8,128)} %sum_near.1), calls=%async_computation.2 | async-start | bytes 131072 | tf_op jit(solution)/shard_map/all_to_all | solution.py:255
  66.1 6.0 %collective-permute-start.1 = (f32[2,128,128]{2,1,0:T(8,128)S(1)}, f32[2,128,128]{2,1,0:T(8,128)S(1)}, u32[]{:S(2)}, u32[]{:S(2)}) collective-permute-start(f32[2,128,128]{2,1,0:T(8,128)S(1)} %get-tuple-element.9), channel_id=1, source_target_pairs={{0,4},{1,5},{2,6},{3,7},{4,0},{5,1},{6,2},{7,3},{8,12},{9,13},{10,... | collective-permute-start | bytes 393224 | tf_op jit(solution)/shard_map/ppermute | solution.py:322
  73.1 10.4 %collective-permute-start.2 = (f32[2,128,256]{2,1,0:T(8,128)S(1)}, f32[2,128,256]{2,1,0:T(8,128)S(1)}, u32[]{:S(2)}, u32[]{:S(2)}) collective-permute-start(f32[2,128,256]{2,1,0:T(8,128)S(1)} %get-tuple-element.13), channel_id=1, source_target_pairs={{0,8},{8,16},{16,24},{24,32},{32,40},{40,48},{48,56},{56,64},{64,7... | collective-permute-start | bytes 786440 | tf_op jit(solution)/shard_map/ppermute | solution.py:342
  78.2 10.9 %all-to-all-start.3 = ((f32[8,16,128]{2,1,0:T(8,128)}), f32[8,16,128]{2,1,0:T(8,128)S(1)}, u32[]{:S(2)}, u32[]{:S(2)}) async-start(f32[8,16,128]{2,1,0:T(8,128)} %sum_far.1), calls=%async_computation.3 | async-start | bytes 131072 | tf_op jit(solution)/shard_map/all_to_all | solution.py:255

commit v5 on v4

--- a/solution.py
+++ b/solution.py
@@ -11,7 +11,7 @@
 from jax.sharding import PartitionSpec as P
 
 PHASE_RATE = 0.05
-ORDER = (0, 6, 3, 5, 1, 7, 2, 4)
+ORDER = (7, 1, 4, 2, 6, 0, 5, 3)
 SUBLANES = 8
 VMEM_BYTES = 48 * 1024 * 1024
 SUM_COST = 100 * 1000 * 1000
@@ -163,7 +163,9 @@
     band = size // slices
     for position in range(2):
         first = (position * half_secs + lax.rem(sec, half_secs)) * band
-        probe_bands[position] = probe_grad[:, pl.ds(pl.multiple_of(first, band), band), :]
+        for k in range(2 * modes):
+            taken = probe_grad[k, pl.ds(pl.multiple_of(first, band), band), :]
+            probe_bands[1 - position, 2 * modes - 1 - k] = taken
 
 
 def aligned(row, size):
@@ -218,7 +220,9 @@
 
 def finish_kernel(owned, received, pieces, obj_grad, probe_grad):
     obj_grad[:, 0] = owned[...] + received[...]
-    probe_grad[...] = pieces[...]
+    count, modes = pieces.shape[0], probe_grad.shape[1]
+    for k in range(count):
+        probe_grad[k // modes, k % modes] = pieces[count - 1 - k]
 
 
 def spread_kernel(blocks, out):
@@ -250,9 +254,12 @@
     return found
 
 
-def exchanged(blocks, bits):
+def exchanged(blocks, bits, last_first=True):
     total = (lax.axis_size("tile") * lax.axis_size("sec")).bit_length() - 1
-    return lax.all_to_all(blocks, AXES, 0, 0, axis_index_groups=groups_of(bits, total))
+    groups = groups_of(bits, total)
+    if last_first:
+        groups = [group[::-1] for group in groups]
+    return lax.all_to_all(blocks, AXES, 0, 0, axis_index_groups=groups)
 
 
 def wave_call(sec, windows, probe, measured, positions=128):
@@ -321,7 +328,7 @@
     half = secs // 2
     other_grad = lax.ppermute(sent_grad, "sec", [(i, (i + half) % secs) for i in range(secs)])
 
-    near, far = (CORE_BIT, Z_BITS[0], X_BIT), Z_BITS[:0:-1]
+    near, far = (CORE_BIT, Z_BITS[0], X_BIT), Z_BITS[1:]
     arrived = exchanged(bands.reshape(-1, band, size), near + (POSITION_BIT,))
     part = summed_to(arrived, 1 << len(far), "sum_near")
     other_grad = lax.optimization_barrier((other_grad, part))[0]
@@ -352,7 +359,7 @@
         out_specs=(vmem, vmem),
         compiler_params=params,
         name="finish",
-    )(owned, received, pieces.reshape(2, modes, band, size))
+    )(owned, received, pieces)
 
 
 def solution(mesh):

time: 90.4 us -> 85.4 us (0.945)
  waiting for transfers between devices: 9.95 us -> 6.31 us
  blocking collectives: 32.6 us -> 31.4 us
    all_to_all x2, waiting for transfers between devices: 6.17 us -> 2.54 us  [exchanged(): return lax.all_to_all(blocks, AXES, 0, 0, axis_index_groups=groups)]
    all_to_all x2, starting transfers between devices: 16.7 us -> 15.3 us  [exchanged(): return lax.all_to_all(blocks, AXES, 0, 0, axis_index_groups=groups)]
    ppermute x1, starting transfers between devices: 4.01 us -> 5.17 us  [per_device(): lax.ppermute(spill, 'tile', [(i, (i + 1) % tiles) for i in range(tiles)])]
    all_to_all x1, blocking collectives: 19.6 us -> 18.7 us  [exchanged(): return lax.all_to_all(blocks, AXES, 0, 0, axis_index_groups=groups)]
  transfers between devices with their start and end apart: 5 -> 5, of which waited for: 3 -> 2; matrix products, arithmetic and copies ran while one was open for 0% -> 0% of each run, Pallas kernels for 3% -> 3%
where the time goes in v5:
time: 85.4 us; the launch traced here: 84.9 us
  starting transfers between devices  31.4 us (37%)
  blocking collectives  31.4 us (37%)
  Pallas kernels  13.1 us (15%)
  waiting for transfers between devices  6.31 us (7%)
  local copies, waits for them, and re-layouts  1.67 us (2%)
  between operations  0.87 us (1%)
    all_to_all x1, blocking collectives, exchanged(): return lax.all_to_all(blocks, AXES, 0, 0, axis_index_groups=groups)  18.7 us
    all_to_all x2, starting transfers between devices, exchanged(): return lax.all_to_all(blocks, AXES, 0, 0, axis_index_groups=groups)  15.3 us
    all_to_all x1, blocking collectives, per_device(): windows = lax.all_to_all(cut, AXES, 0, 0, axis_index_groups=ranks)  12.7 us
    ppermute x1, starting transfers between devices, per_device(): lax.ppermute(own, 'tile', [(i, (i - 1) % tiles) for i in range(tiles)])  8.79 us
    pallas_call x1, Pallas kernels, wave_call(): pl.pallas_call(functools.partial(wave_kernel, 1.0 / positions), out_shape...  8.5 us
    ppermute x1, starting transfers between devices, per_device(): lax.ppermute(spill, 'tile', [(i, (i + 1) % tiles) for i in range(tiles)])  5.17 us
    ppermute x1, waiting for transfers between devices, per_device(): lax.ppermute(sent_grad, 'sec', [(i, (i + half) % secs) for i in range(sec...  3.76 us
    all_to_all x2, waiting for transfers between devices, exchanged(): return lax.all_to_all(blocks, AXES, 0, 0, axis_index_groups=groups)  2.54 us
  transfers between devices with their start and end apart: 5, of which 2 were waited for; matrix products, arithmetic and copies ran while one was open for 0% of the time, Pallas kernels for 3%

profile of v5, /device:TPU:1, one launch (start us, length us, event | category | flops | bytes accessed | tf_op | source)
XLA Modules:
  0.0 84.9 jit_solution(11402663497222291424)
XLA Ops:
  0.6 8.8 %collective-permute-start = (f32[2,128,256]{2,1,0:T(8,128)}, f32[2,128,256]{2,1,0:T(8,128)S(1)}, u32[]{:S(2)}, u32[]{:S(2)}) collective-permute-start(f32[2,128,256]{2,1,0:T(8,128)} %bitcast.3), channel_id=1, source_target_pairs={{0,504},{8,0},{16,8},{24,16},{32,24},{40,32},{48,40},{56,48},{64,5... | collective-permute-start | bytes 786440 | tf_op jit(solution)/shard_map/ppermute | solution.py:305
  9.4 0.0 copy-start.11
  9.4 0.0 copy-start.12
  9.4 0.6 copy-done.11
  10.1 0.0 copy-done.12
  10.1 0.0 copy-start.1
  10.1 0.9 %copy-done.1 = f32[2,1,128,256]{3,2,1,0:T(8,128)S(1)} copy-done((f32[2,1,128,256]{3,2,1,0:T(8,128)S(1)}, f32[2,1,128,256]{3,2,1,0:T(8,128)}, u32[]{:S(2)}) %copy-start.1) | copy-done | bytes 262168
  11.1 0.8 own_windows.1.own
  11.8 0.0 collective-permute-done.rim
  11.8 0.9 %cut_windows.1 = f32[8,2,128,128]{3,2,1,0:T(8,128)S(1)} custom-call(s32[1]{0:T(128)} %bitcast.sec_ref, s32[2]{0:T(128)S(1)} %copy-done.11, s32[2]{0:T(128)S(1)} %copy-done.12, f32[2,2,128,128]{3,2,1,0:T(8,128)S(1)} %own_windows.1.own, f32[2,128,256]{2,1,0:T(8,128)S(1)} %collective-permute-done.rim), custom_call_target="tpu_custom_call" | custom-call | tf_op jit(solution)/shard_map/cut_windows/pallas_call | solution.py:314
  12.8 0.0 copy-start
  12.8 0.0 copy-start.2
  12.8 0.0 copy-start.3
  12.8 0.0 copy-start.4
  12.8 0.0 copy-start.5
  12.8 0.0 copy-start.6
  12.8 0.0 copy-start.7
  12.8 0.0 copy-start.8
  12.9 0.0 copy-start.9
  12.9 0.0 copy-start.10
  12.9 12.7 %all_to_all.20.windows = f32[8,2,128,128]{3,2,1,0:T(8,128)S(1)} all-to-all(f32[8,2,128,128]{3,2,1,0:T(8,128)S(1)} %cut_windows.1), channel_id=1, replica_groups={{7,1,4,2,6,0,5,3},{15,9,12,10,14,8,13,11},{23,17,20,18,22,16,21,19},{31..., dimensions={0} | all-to-all | bytes 2097152 | tf_op jit(solution)/shard_map/all_to_all | solution.py:323
  25.6 0.0 copy-done
  25.6 0.0 copy-done.2
  25.6 0.0 copy-done.3
  25.6 0.0 copy-done.4
  25.6 0.0 copy-done.5
  25.6 0.0 copy-done.6
  25.7 0.0 copy-done.7
  25.7 0.0 copy-done.8
  25.7 0.0 copy-done.9
  25.7 0.0 copy-done.10
  25.7 8.5 %wave_gradients.1 = (f32[2,128,128]{2,1,0:T(8,128)S(1)}, f32[2,128,128]{2,1,0:T(8,128)S(1)}, f32[2,8,16,128]{3,2,1,0:T(8,128)S(1)}) custom-call(s32[1]{0:T(128)} %bitcast.sec_ref, f32[8,2,128,128]{3,2,1,0:T(8,128)S(1)} %all_to_all.20.windows, f32[2,4,128,128]{3,2,1,0:T(8,128)S(1)} %copy-done, f32[2,128,128]{2,1,0:T(8,128)S(1)} %copy-done.2, ...), custom_call_target="tpu_custom_call" | custom-call | tf_op jit(solution)/shard_map/wave_gradients/pallas_call | solution.py:273
  34.2 18.7 %all_to_all.21.blocks = f32[16,16,128]{2,1,0:T(8,128)S(1)} all-to-all(f32[16,16,128]{2,1,0:T(8,128)S(1)} %bitcast.5), channel_id=1, replica_groups={{284,276,268,260,28,20,12,4,280,272,264,256,24,16,8,0},{285,277,269,261..., dimensions={0} | all-to-all | bytes 262144 | tf_op jit(solution)/shard_map/all_to_all | solution.py:262
  52.9 0.6 sum_near.1
  53.6 9.6 %all-to-all-start.2 = ((f32[8,16,128]{2,1,0:T(8,128)}), f32[8,16,128]{2,1,0:T(8,128)S(1)}, u32[]{:S(2)}, u32[]{:S(2)}) async-start(f32[8,16,128]{2,1,0:T(8,128)} %sum_near.1), calls=%async_computation.2 | async-start | bytes 131072 | tf_op jit(solution)/shard_map/all_to_all | solution.py:262
  63.2 2.2 %collective-permute-start.1 = (f32[2,128,128]{2,1,0:T(8,128)S(1)}, f32[2,128,128]{2,1,0:T(8,128)S(1)}, u32[]{:S(2)}, u32[]{:S(2)}) collective-permute-start(f32[2,128,128]{2,1,0:T(8,128)S(1)} %get-tuple-element.9), channel_id=1, source_target_pairs={{0,4},{1,5},{2,6},{3,7},{4,0},{5,1},{6,2},{7,3},{8,12},{9,13},{10,... | collective-permute-start | bytes 393224 | tf_op jit(solution)/shard_map/ppermute | solution.py:329
  65.4 0.1 pad_add_fusion.sec_ref
  65.4 3.8 %collective-permute-done.1.other_grad = f32[2,128,128]{2,1,0:T(8,128)S(1)} collective-permute-done((f32[2,128,128]{2,1,0:T(8,128)S(1)}, f32[2,128,128]{2,1,0:T(8,128)S(1)}, u32[]{:S(2)}, u32[]{:S(2)}) %collective-permute-start.1) | collective-permute-done | bytes 131104 | tf_op jit(solution)/shard_map/ppermute | solution.py:329
  69.2 0.9 %scatter_windows.1 = (f32[2,128,256]{2,1,0:T(8,128)S(1)}, f32[2,128,256]{2,1,0:T(8,128)S(1)}) custom-call(s32[2]{0:T(128)S(1)} %pad_add_fusion.sec_ref, s32[2]{0:T(128)S(1)} %copy-done.11, s32[2]{0:T(128)S(1)} %copy-done.12, f32[2,128,128]{2,1,0:T(8,128)S(1)} %get-tuple-element.8.own_grad, f32[2,128,128]{2,1,0:T(8,128)S(1)} %collective-permute-done.1.other_grad), custom_call_target="tpu_custom_call" | custom-call | tf_op jit(solution)/shard_map/scatter_windows/pallas_call | solution.py:337
  70.1 5.2 %collective-permute-start.2 = (f32[2,128,256]{2,1,0:T(8,128)S(1)}, f32[2,128,256]{2,1,0:T(8,128)S(1)}, u32[]{:S(2)}, u32[]{:S(2)}) collective-permute-start(f32[2,128,256]{2,1,0:T(8,128)S(1)} %get-tuple-element.13), channel_id=1, source_target_pairs={{0,8},{8,16},{16,24},{24,32},{32,40},{40,48},{48,56},{56,64},{64,7... | collective-permute-start | bytes 786440 | tf_op jit(solution)/shard_map/ppermute | solution.py:349
  75.3 0.0 all-to-all-done.2.blocks
  75.3 0.6 sum_far.1
  75.9 5.7 %all-to-all-start.3 = ((f32[8,16,128]{2,1,0:T(8,128)}), f32[8,16,128]{2,1,0:T(8,128)S(1)}, u32[]{:S(2)}, u32[]{:S(2)}) async-start(f32[8,16,128]{2,1,0:T(8,128)} %sum_far.1), calls=%async_computation.3 | async-start | bytes 131072 | tf_op jit(solution)/shard_map/all_to_all | solution.py:262
  81.6 0.0 collective-permute-done.2.received
  81.6 2.5 %all-to-all-done.3.pieces = f32[8,16,128]{2,1,0:T(8,128)S(1)} async-done(((f32[8,16,128]{2,1,0:T(8,128)}), f32[8,16,128]{2,1,0:T(8,128)S(1)}, u32[]{:S(2)}, u32[]{:S(2)}) %all-to-all-start.3) | async-done | bytes 65568 | tf_op jit(solution)/shard_map/all_to_all | solution.py:262
  84.2 0.7 finish.1
Async XLA Ops:
  0.6 11.2 %collective-permute-start = (f32[2,128,256]{2,1,0:T(8,128)}, f32[2,128,256]{2,1,0:T(8,128)S(1)}, u32[]{:S(2)}, u32[]{:S(2)}) collective-permute-start(f32[2,128,256]{2,1,0:T(8,128)} %bitcast.3), channel_id=1, source_target_pairs={{0,504},{8,0},{16,8},{24,16},{32,24},{40,32},{48,40},{56,48},{64,5... | collective-permute-start | bytes 786440 | tf_op jit(solution)/shard_map/ppermute | solution.py:305
  9.4 0.7 copy-start.11
  9.4 0.7 copy-start.12
  10.1 0.9 %copy-start.1 = (f32[2,1,128,256]{3,2,1,0:T(8,128)S(1)}, f32[2,1,128,256]{3,2,1,0:T(8,128)}, u32[]{:S(2)}) copy-start(f32[2,1,128,256]{3,2,1,0:T(8,128)} %param.13) | copy-start | bytes 786436
  12.8 12.9 %copy-start = (f32[2,4,128,128]{3,2,1,0:T(8,128)S(1)}, f32[2,4,128,128]{3,2,1,0:T(8,128)}, u32[]{:S(2)}) copy-start(f32[2,4,128,128]{3,2,1,0:T(8,128)} %probe.1) | copy-start | bytes 1572868
  12.8 12.9 %copy-start.2 = (f32[2,128,128]{2,1,0:T(8,128)S(1)}, f32[2,128,128]{2,1,0:T(8,128)}, u32[]{:S(2)}) copy-start(f32[2,128,128]{2,1,0:T(8,128)} %measured.1) | copy-start | bytes 393220
  12.8 12.8 %copy-start.3 = (bf16[256,256]{1,0:T(8,128)(2,1)S(1)}, bf16[256,256]{1,0:T(8,128)(2,1)}, u32[]{:S(2)}) copy-start(bf16[256,256]{1,0:T(8,128)(2,1)} %constant.22.clone.prop_high) | copy-start | bytes 393220
  12.8 12.8 %copy-start.4 = (bf16[256,256]{1,0:T(8,128)(2,1)S(1)}, bf16[256,256]{1,0:T(8,128)(2,1)}, u32[]{:S(2)}) copy-start(bf16[256,256]{1,0:T(8,128)(2,1)} %constant.23.clone.prop_low) | copy-start | bytes 393220
  12.8 12.8 %copy-start.5 = (bf16[256,256]{1,0:T(8,128)(2,1)S(1)}, bf16[256,256]{1,0:T(8,128)(2,1)}, u32[]{:S(2)}) copy-start(bf16[256,256]{1,0:T(8,128)(2,1)} %constant.24.clone.back_high) | copy-start | bytes 393220
  12.8 12.8 %copy-start.6 = (bf16[256,256]{1,0:T(8,128)(2,1)S(1)}, bf16[256,256]{1,0:T(8,128)(2,1)}, u32[]{:S(2)}) copy-start(bf16[256,256]{1,0:T(8,128)(2,1)} %constant.25.clone.back_low) | copy-start | bytes 393220
  12.8 12.8 %copy-start.7 = (bf16[256,256]{1,0:T(8,128)(2,1)S(1)}, bf16[256,256]{1,0:T(8,128)(2,1)}, u32[]{:S(2)}) copy-start(bf16[256,256]{1,0:T(8,128)(2,1)} %constant.26.clone.four_high) | copy-start | bytes 393220
  12.8 12.8 %copy-start.8 = (bf16[256,256]{1,0:T(8,128)(2,1)S(1)}, bf16[256,256]{1,0:T(8,128)(2,1)}, u32[]{:S(2)}) copy-start(bf16[256,256]{1,0:T(8,128)(2,1)} %constant.27.clone.four_low) | copy-start | bytes 393220
  12.9 12.8 %copy-start.9 = (bf16[256,256]{1,0:T(8,128)(2,1)S(1)}, bf16[256,256]{1,0:T(8,128)(2,1)}, u32[]{:S(2)}) copy-start(bf16[256,256]{1,0:T(8,128)(2,1)} %constant.28.clone.inv_high) | copy-start | bytes 393220
  12.9 12.8 %copy-start.10 = (bf16[256,256]{1,0:T(8,128)(2,1)S(1)}, bf16[256,256]{1,0:T(8,128)(2,1)}, u32[]{:S(2)}) copy-start(bf16[256,256]{1,0:T(8,128)(2,1)} %constant.29.clone.inv_low) | copy-start | bytes 393220
  53.6 21.7 %all-to-all-start.2 = ((f32[8,16,128]{2,1,0:T(8,128)}), f32[8,16,128]{2,1,0:T(8,128)S(1)}, u32[]{:S(2)}, u32[]{:S(2)}) async-start(f32[8,16,128]{2,1,0:T(8,128)} %sum_near.1), calls=%async_computation.2 | async-start | bytes 131072 | tf_op jit(solution)/shard_map/all_to_all | solution.py:262
  63.2 6.0 %collective-permute-start.1 = (f32[2,128,128]{2,1,0:T(8,128)S(1)}, f32[2,128,128]{2,1,0:T(8,128)S(1)}, u32[]{:S(2)}, u32[]{:S(2)}) collective-permute-start(f32[2,128,128]{2,1,0:T(8,128)S(1)} %get-tuple-element.9), channel_id=1, source_target_pairs={{0,4},{1,5},{2,6},{3,7},{4,0},{5,1},{6,2},{7,3},{8,12},{9,13},{10,... | collective-permute-start | bytes 393224 | tf_op jit(solution)/shard_map/ppermute | solution.py:329
  70.1 11.5 %collective-permute-start.2 = (f32[2,128,256]{2,1,0:T(8,128)S(1)}, f32[2,128,256]{2,1,0:T(8,128)S(1)}, u32[]{:S(2)}, u32[]{:S(2)}) collective-permute-start(f32[2,128,256]{2,1,0:T(8,128)S(1)} %get-tuple-element.13), channel_id=1, source_target_pairs={{0,8},{8,16},{16,24},{24,32},{32,40},{40,48},{48,56},{56,64},{64,7... | collective-permute-start | bytes 786440 | tf_op jit(solution)/shard_map/ppermute | solution.py:349
  75.9 8.2 %all-to-all-start.3 = ((f32[8,16,128]{2,1,0:T(8,128)}), f32[8,16,128]{2,1,0:T(8,128)S(1)}, u32[]{:S(2)}, u32[]{:S(2)}) async-start(f32[8,16,128]{2,1,0:T(8,128)} %sum_far.1), calls=%async_computation.3 | async-start | bytes 131072 | tf_op jit(solution)/shard_map/all_to_all | solution.py:262

commit v6 on v5

--- a/solution.py
+++ b/solution.py
@@ -11,7 +11,7 @@
 from jax.sharding import PartitionSpec as P
 
 PHASE_RATE = 0.05
-ORDER = (7, 1, 4, 2, 6, 0, 5, 3)
+ORDER = (7, 6, 5, 4, 3, 2, 1, 0)
 SUBLANES = 8
 VMEM_BYTES = 48 * 1024 * 1024
 SUM_COST = 100 * 1000 * 1000
@@ -222,7 +222,7 @@
     obj_grad[:, 0] = owned[...] + received[...]
     count, modes = pieces.shape[0], probe_grad.shape[1]
     for k in range(count):
-        probe_grad[k // modes, k % modes] = pieces[count - 1 - k]
+        probe_grad[k // modes, k % modes] = pieces[count - 1 - (k ^ 1)]
 
 
 def spread_kernel(blocks, out):
@@ -254,11 +254,10 @@
     return found
 
 
-def exchanged(blocks, bits, last_first=True):
+def exchanged(blocks, bits, flip=0):
     total = (lax.axis_size("tile") * lax.axis_size("sec")).bit_length() - 1
     groups = groups_of(bits, total)
-    if last_first:
-        groups = [group[::-1] for group in groups]
+    groups = [[group[place ^ flip] for place in reversed(range(len(group)))] for group in groups]
     return lax.all_to_all(blocks, AXES, 0, 0, axis_index_groups=groups)
 
 
@@ -348,7 +347,7 @@
     )(jnp.stack([sec, jnp.int32(secs)]), row_offset, col_offset, own_grad, other_grad)
     received = lax.ppermute(spill, "tile", [(i, (i + 1) % tiles) for i in range(tiles)])
 
-    pieces = exchanged(summed_to(arrived, 1 << len(near), "sum_far"), near)
+    pieces = exchanged(summed_to(arrived, 1 << len(near), "sum_far"), near, 1)
     return pl.pallas_call(
         finish_kernel,
         out_shape=(

time: 85.4 us -> 84.8 us (level)
  no operation moved by 1% of the time
where the time goes in v6:
time: 84.8 us; the launch traced here: 84.4 us
  blocking collectives  31.4 us (37%)
  starting transfers between devices  31.1 us (37%)
  Pallas kernels  13.1 us (15%)
  waiting for transfers between devices  6.22 us (7%)
  local copies, waits for them, and re-layouts  1.67 us (2%)
  between operations  0.87 us (1%)
    all_to_all x1, blocking collectives, exchanged(): return lax.all_to_all(blocks, AXES, 0, 0, axis_index_groups=groups)  18.7 us
    all_to_all x2, starting transfers between devices, exchanged(): return lax.all_to_all(blocks, AXES, 0, 0, axis_index_groups=groups)  14.9 us
    all_to_all x1, blocking collectives, per_device(): windows = lax.all_to_all(cut, AXES, 0, 0, axis_index_groups=ranks)  12.7 us
    ppermute x1, starting transfers between devices, per_device(): lax.ppermute(own, 'tile', [(i, (i - 1) % tiles) for i in range(tiles)])  8.79 us
    pallas_call x1, Pallas kernels, wave_call(): pl.pallas_call(functools.partial(wave_kernel, 1.0 / positions), out_shape...  8.48 us
    ppermute x1, starting transfers between devices, per_device(): lax.ppermute(spill, 'tile', [(i, (i + 1) % tiles) for i in range(tiles)])  5.17 us
    ppermute x1, waiting for transfers between devices, per_device(): lax.ppermute(sent_grad, 'sec', [(i, (i + half) % secs) for i in range(sec...  3.76 us
    all_to_all x2, waiting for transfers between devices, exchanged(): return lax.all_to_all(blocks, AXES, 0, 0, axis_index_groups=groups)  2.45 us
  transfers between devices with their start and end apart: 5, of which 2 were waited for; matrix products, arithmetic and copies ran while one was open for 0% of the time, Pallas kernels for 3%

profile of v6, /device:TPU:1, one launch (start us, length us, event | category | flops | bytes accessed | tf_op | source)
XLA Modules:
  0.0 84.4 jit_solution(13958310464181031546)
XLA Ops:
  0.6 8.8 %collective-permute-start = (f32[2,128,256]{2,1,0:T(8,128)}, f32[2,128,256]{2,1,0:T(8,128)S(1)}, u32[]{:S(2)}, u32[]{:S(2)}) collective-permute-start(f32[2,128,256]{2,1,0:T(8,128)} %bitcast.3), channel_id=1, source_target_pairs={{0,504},{8,0},{16,8},{24,16},{32,24},{40,32},{48,40},{56,48},{64,5... | collective-permute-start | bytes 786440 | tf_op jit(solution)/shard_map/ppermute | solution.py:304
  9.4 0.0 copy-start.11
  9.4 0.0 copy-start.12
  9.4 0.6 copy-done.11
  10.1 0.0 copy-done.12
  10.1 0.0 copy-start.1
  10.1 0.9 %copy-done.1 = f32[2,1,128,256]{3,2,1,0:T(8,128)S(1)} copy-done((f32[2,1,128,256]{3,2,1,0:T(8,128)S(1)}, f32[2,1,128,256]{3,2,1,0:T(8,128)}, u32[]{:S(2)}) %copy-start.1) | copy-done | bytes 262168
  11.1 0.8 own_windows.1.own
  11.8 0.0 collective-permute-done.rim
  11.8 0.9 %cut_windows.1 = f32[8,2,128,128]{3,2,1,0:T(8,128)S(1)} custom-call(s32[1]{0:T(128)} %bitcast.sec_ref, s32[2]{0:T(128)S(1)} %copy-done.11, s32[2]{0:T(128)S(1)} %copy-done.12, f32[2,2,128,128]{3,2,1,0:T(8,128)S(1)} %own_windows.1.own, f32[2,128,256]{2,1,0:T(8,128)S(1)} %collective-permute-done.rim), custom_call_target="tpu_custom_call" | custom-call | tf_op jit(solution)/shard_map/cut_windows/pallas_call | solution.py:313
  12.8 0.0 copy-start
  12.8 0.0 copy-start.2
  12.8 0.0 copy-start.3
  12.8 0.0 copy-start.4
  12.8 0.0 copy-start.5
  12.8 0.0 copy-start.6
  12.8 0.0 copy-start.7
  12.8 0.0 copy-start.8
  12.9 0.0 copy-start.9
  12.9 0.0 copy-start.10
  12.9 12.7 %all_to_all.20.windows = f32[8,2,128,128]{3,2,1,0:T(8,128)S(1)} all-to-all(f32[8,2,128,128]{3,2,1,0:T(8,128)S(1)} %cut_windows.1), channel_id=1, replica_groups={{7,6,5,4,3,2,1,0},{15,14,13,12,11,10,9,8},{23,22,21,20,19,18,17,16},{31..., dimensions={0} | all-to-all | bytes 2097152 | tf_op jit(solution)/shard_map/all_to_all | solution.py:322
  25.6 0.0 copy-done
  25.6 0.0 copy-done.2
  25.6 0.0 copy-done.3
  25.6 0.0 copy-done.4
  25.6 0.0 copy-done.5
  25.6 0.0 copy-done.6
  25.7 0.0 copy-done.7
  25.7 0.0 copy-done.8
  25.7 0.0 copy-done.9
  25.7 0.0 copy-done.10
  25.7 8.5 %wave_gradients.1 = (f32[2,128,128]{2,1,0:T(8,128)S(1)}, f32[2,128,128]{2,1,0:T(8,128)S(1)}, f32[2,8,16,128]{3,2,1,0:T(8,128)S(1)}) custom-call(s32[1]{0:T(128)} %bitcast.sec_ref, f32[8,2,128,128]{3,2,1,0:T(8,128)S(1)} %all_to_all.20.windows, f32[2,4,128,128]{3,2,1,0:T(8,128)S(1)} %copy-done, f32[2,128,128]{2,1,0:T(8,128)S(1)} %copy-done.2, ...), custom_call_target="tpu_custom_call" | custom-call | tf_op jit(solution)/shard_map/wave_gradients/pallas_call | solution.py:272
  34.2 18.7 %all_to_all.21.blocks = f32[16,16,128]{2,1,0:T(8,128)S(1)} all-to-all(f32[16,16,128]{2,1,0:T(8,128)S(1)} %bitcast.5), channel_id=1, replica_groups={{284,276,268,260,28,20,12,4,280,272,264,256,24,16,8,0},{285,277,269,261..., dimensions={0} | all-to-all | bytes 262144 | tf_op jit(solution)/shard_map/all_to_all | solution.py:261
  52.8 0.6 sum_near.1
  53.5 9.5 %all-to-all-start.2 = ((f32[8,16,128]{2,1,0:T(8,128)}), f32[8,16,128]{2,1,0:T(8,128)S(1)}, u32[]{:S(2)}, u32[]{:S(2)}) async-start(f32[8,16,128]{2,1,0:T(8,128)} %sum_near.1), calls=%async_computation.2 | async-start | bytes 131072 | tf_op jit(solution)/shard_map/all_to_all | solution.py:261
  63.0 2.2 %collective-permute-start.1 = (f32[2,128,128]{2,1,0:T(8,128)S(1)}, f32[2,128,128]{2,1,0:T(8,128)S(1)}, u32[]{:S(2)}, u32[]{:S(2)}) collective-permute-start(f32[2,128,128]{2,1,0:T(8,128)S(1)} %get-tuple-element.9), channel_id=1, source_target_pairs={{0,4},{1,5},{2,6},{3,7},{4,0},{5,1},{6,2},{7,3},{8,12},{9,13},{10,... | collective-permute-start | bytes 393224 | tf_op jit(solution)/shard_map/ppermute | solution.py:328
  65.1 0.1 pad_add_fusion.sec_ref
  65.2 3.8 %collective-permute-done.1.other_grad = f32[2,128,128]{2,1,0:T(8,128)S(1)} collective-permute-done((f32[2,128,128]{2,1,0:T(8,128)S(1)}, f32[2,128,128]{2,1,0:T(8,128)S(1)}, u32[]{:S(2)}, u32[]{:S(2)}) %collective-permute-start.1) | collective-permute-done | bytes 131104 | tf_op jit(solution)/shard_map/ppermute | solution.py:328
  69.0 0.9 %scatter_windows.1 = (f32[2,128,256]{2,1,0:T(8,128)S(1)}, f32[2,128,256]{2,1,0:T(8,128)S(1)}) custom-call(s32[2]{0:T(128)S(1)} %pad_add_fusion.sec_ref, s32[2]{0:T(128)S(1)} %copy-done.11, s32[2]{0:T(128)S(1)} %copy-done.12, f32[2,128,128]{2,1,0:T(8,128)S(1)} %get-tuple-element.8.own_grad, f32[2,128,128]{2,1,0:T(8,128)S(1)} %collective-permute-done.1.other_grad), custom_call_target="tpu_custom_call" | custom-call | tf_op jit(solution)/shard_map/scatter_windows/pallas_call | solution.py:336
  69.9 5.2 %collective-permute-start.2 = (f32[2,128,256]{2,1,0:T(8,128)S(1)}, f32[2,128,256]{2,1,0:T(8,128)S(1)}, u32[]{:S(2)}, u32[]{:S(2)}) collective-permute-start(f32[2,128,256]{2,1,0:T(8,128)S(1)} %get-tuple-element.13), channel_id=1, source_target_pairs={{0,8},{8,16},{16,24},{24,32},{32,40},{40,48},{48,56},{56,64},{64,7... | collective-permute-start | bytes 786440 | tf_op jit(solution)/shard_map/ppermute | solution.py:348
  75.0 0.0 all-to-all-done.2.blocks
  75.1 0.6 sum_far.1
  75.7 5.5 %all-to-all-start.3 = ((f32[8,16,128]{2,1,0:T(8,128)}), f32[8,16,128]{2,1,0:T(8,128)S(1)}, u32[]{:S(2)}, u32[]{:S(2)}) async-start(f32[8,16,128]{2,1,0:T(8,128)} %sum_far.1), calls=%async_computation.3 | async-start | bytes 131072 | tf_op jit(solution)/shard_map/all_to_all | solution.py:261
  81.2 0.0 collective-permute-done.2.received
  81.2 2.4 %all-to-all-done.3.pieces = f32[8,16,128]{2,1,0:T(8,128)S(1)} async-done(((f32[8,16,128]{2,1,0:T(8,128)}), f32[8,16,128]{2,1,0:T(8,128)S(1)}, u32[]{:S(2)}, u32[]{:S(2)}) %all-to-all-start.3) | async-done | bytes 65568 | tf_op jit(solution)/shard_map/all_to_all | solution.py:261
  83.6 0.7 finish.1
Async XLA Ops:
  0.6 11.2 %collective-permute-start = (f32[2,128,256]{2,1,0:T(8,128)}, f32[2,128,256]{2,1,0:T(8,128)S(1)}, u32[]{:S(2)}, u32[]{:S(2)}) collective-permute-start(f32[2,128,256]{2,1,0:T(8,128)} %bitcast.3), channel_id=1, source_target_pairs={{0,504},{8,0},{16,8},{24,16},{32,24},{40,32},{48,40},{56,48},{64,5... | collective-permute-start | bytes 786440 | tf_op jit(solution)/shard_map/ppermute | solution.py:304
  9.4 0.7 copy-start.11
  9.4 0.7 copy-start.12
  10.1 0.9 %copy-start.1 = (f32[2,1,128,256]{3,2,1,0:T(8,128)S(1)}, f32[2,1,128,256]{3,2,1,0:T(8,128)}, u32[]{:S(2)}) copy-start(f32[2,1,128,256]{3,2,1,0:T(8,128)} %param.13) | copy-start | bytes 786436
  12.8 12.9 %copy-start = (f32[2,4,128,128]{3,2,1,0:T(8,128)S(1)}, f32[2,4,128,128]{3,2,1,0:T(8,128)}, u32[]{:S(2)}) copy-start(f32[2,4,128,128]{3,2,1,0:T(8,128)} %probe.1) | copy-start | bytes 1572868
  12.8 12.8 %copy-start.2 = (f32[2,128,128]{2,1,0:T(8,128)S(1)}, f32[2,128,128]{2,1,0:T(8,128)}, u32[]{:S(2)}) copy-start(f32[2,128,128]{2,1,0:T(8,128)} %measured.1) | copy-start | bytes 393220
  12.8 12.8 %copy-start.3 = (bf16[256,256]{1,0:T(8,128)(2,1)S(1)}, bf16[256,256]{1,0:T(8,128)(2,1)}, u32[]{:S(2)}) copy-start(bf16[256,256]{1,0:T(8,128)(2,1)} %constant.22.clone.prop_high) | copy-start | bytes 393220
  12.8 12.8 %copy-start.4 = (bf16[256,256]{1,0:T(8,128)(2,1)S(1)}, bf16[256,256]{1,0:T(8,128)(2,1)}, u32[]{:S(2)}) copy-start(bf16[256,256]{1,0:T(8,128)(2,1)} %constant.23.clone.prop_low) | copy-start | bytes 393220
  12.8 12.8 %copy-start.5 = (bf16[256,256]{1,0:T(8,128)(2,1)S(1)}, bf16[256,256]{1,0:T(8,128)(2,1)}, u32[]{:S(2)}) copy-start(bf16[256,256]{1,0:T(8,128)(2,1)} %constant.24.clone.back_high) | copy-start | bytes 393220
  12.8 12.8 %copy-start.6 = (bf16[256,256]{1,0:T(8,128)(2,1)S(1)}, bf16[256,256]{1,0:T(8,128)(2,1)}, u32[]{:S(2)}) copy-start(bf16[256,256]{1,0:T(8,128)(2,1)} %constant.25.clone.back_low) | copy-start | bytes 393220
  12.8 12.8 %copy-start.7 = (bf16[256,256]{1,0:T(8,128)(2,1)S(1)}, bf16[256,256]{1,0:T(8,128)(2,1)}, u32[]{:S(2)}) copy-start(bf16[256,256]{1,0:T(8,128)(2,1)} %constant.26.clone.four_high) | copy-start | bytes 393220
  12.8 12.8 %copy-start.8 = (bf16[256,256]{1,0:T(8,128)(2,1)S(1)}, bf16[256,256]{1,0:T(8,128)(2,1)}, u32[]{:S(2)}) copy-start(bf16[256,256]{1,0:T(8,128)(2,1)} %constant.27.clone.four_low) | copy-start | bytes 393220
  12.9 12.8 %copy-start.9 = (bf16[256,256]{1,0:T(8,128)(2,1)S(1)}, bf16[256,256]{1,0:T(8,128)(2,1)}, u32[]{:S(2)}) copy-start(bf16[256,256]{1,0:T(8,128)(2,1)} %constant.28.clone.inv_high) | copy-start | bytes 393220
  12.9 12.8 %copy-start.10 = (bf16[256,256]{1,0:T(8,128)(2,1)S(1)}, bf16[256,256]{1,0:T(8,128)(2,1)}, u32[]{:S(2)}) copy-start(bf16[256,256]{1,0:T(8,128)(2,1)} %constant.29.clone.inv_low) | copy-start | bytes 393220
  53.5 21.6 %all-to-all-start.2 = ((f32[8,16,128]{2,1,0:T(8,128)}), f32[8,16,128]{2,1,0:T(8,128)S(1)}, u32[]{:S(2)}, u32[]{:S(2)}) async-start(f32[8,16,128]{2,1,0:T(8,128)} %sum_near.1), calls=%async_computation.2 | async-start | bytes 131072 | tf_op jit(solution)/shard_map/all_to_all | solution.py:261
  63.0 6.0 %collective-permute-start.1 = (f32[2,128,128]{2,1,0:T(8,128)S(1)}, f32[2,128,128]{2,1,0:T(8,128)S(1)}, u32[]{:S(2)}, u32[]{:S(2)}) collective-permute-start(f32[2,128,128]{2,1,0:T(8,128)S(1)} %get-tuple-element.9), channel_id=1, source_target_pairs={{0,4},{1,5},{2,6},{3,7},{4,0},{5,1},{6,2},{7,3},{8,12},{9,13},{10,... | collective-permute-start | bytes 393224 | tf_op jit(solution)/shard_map/ppermute | solution.py:328
  69.9 11.3 %collective-permute-start.2 = (f32[2,128,256]{2,1,0:T(8,128)S(1)}, f32[2,128,256]{2,1,0:T(8,128)S(1)}, u32[]{:S(2)}, u32[]{:S(2)}) collective-permute-start(f32[2,128,256]{2,1,0:T(8,128)S(1)} %get-tuple-element.13), channel_id=1, source_target_pairs={{0,8},{8,16},{16,24},{24,32},{32,40},{40,48},{48,56},{56,64},{64,7... | collective-permute-start | bytes 786440 | tf_op jit(solution)/shard_map/ppermute | solution.py:348
  75.7 7.9 %all-to-all-start.3 = ((f32[8,16,128]{2,1,0:T(8,128)}), f32[8,16,128]{2,1,0:T(8,128)S(1)}, u32[]{:S(2)}, u32[]{:S(2)}) async-start(f32[8,16,128]{2,1,0:T(8,128)} %sum_far.1), calls=%async_computation.3 | async-start | bytes 131072 | tf_op jit(solution)/shard_map/all_to_all | solution.py:261

commit v7 on v6

--- a/solution.py
+++ b/solution.py
@@ -109,13 +109,12 @@
     four, inv = (four_high, four_low), (inv_high, inv_low)
     sec = sec_ref[0]
     half_secs = slices // 2
-    waves[0] = probe[...]
 
     def exits(step):
         win_re, win_im = windows[ORDER.index(step), 0], windows[ORDER.index(step), 1]
         found = []
         for k in range(modes):
-            wave_re, wave_im = waves[step, 0, k], waves[step, 1, k]
+            wave_re, wave_im = (waves[step, 0, k], waves[step, 1, k]) if step else (probe[0, k], probe[1, k])
             found.append((wave_re * win_re - wave_im * win_im, wave_re * win_im + wave_im * win_re))
         return found
 
@@ -133,7 +132,7 @@
     def window_grad(step):
         total_re = total_im = 0.0
         for k in range(modes):
-            wave_re, wave_im = waves[step, 0, k], waves[step, 1, k]
+            wave_re, wave_im = (waves[step, 0, k], waves[step, 1, k]) if step else (probe[0, k], probe[1, k])
             grad_re, grad_im = grads[0, k], grads[1, k]
             total_re = total_re + (wave_re * grad_re + wave_im * grad_im)
             total_im = total_im + (wave_re * grad_im - wave_im * grad_re)

time: 84.8 us -> 84.8 us (level)
  no operation moved by 1% of the time
where the time goes in v7:
time: 84.8 us; the launch traced here: 84.4 us
  blocking collectives  31.4 us (37%)
  starting transfers between devices  31.1 us (37%)
  Pallas kernels  13.1 us (15%)
  waiting for transfers between devices  6.22 us (7%)
  local copies, waits for them, and re-layouts  1.67 us (2%)
  between operations  0.87 us (1%)
    all_to_all x1, blocking collectives, exchanged(): return lax.all_to_all(blocks, AXES, 0, 0, axis_index_groups=groups)  18.7 us
    all_to_all x2, starting transfers between devices, exchanged(): return lax.all_to_all(blocks, AXES, 0, 0, axis_index_groups=groups)  14.9 us
    all_to_all x1, blocking collectives, per_device(): windows = lax.all_to_all(cut, AXES, 0, 0, axis_index_groups=ranks)  12.7 us
    ppermute x1, starting transfers between devices, per_device(): lax.ppermute(own, 'tile', [(i, (i - 1) % tiles) for i in range(tiles)])  8.79 us
    pallas_call x1, Pallas kernels, wave_call(): pl.pallas_call(functools.partial(wave_kernel, 1.0 / positions), out_shape...  8.48 us
    ppermute x1, starting transfers between devices, per_device(): lax.ppermute(spill, 'tile', [(i, (i + 1) % tiles) for i in range(tiles)])  5.17 us
    ppermute x1, waiting for transfers between devices, per_device(): lax.ppermute(sent_grad, 'sec', [(i, (i + half) % secs) for i in range(sec...  3.76 us
    all_to_all x2, waiting for transfers between devices, exchanged(): return lax.all_to_all(blocks, AXES, 0, 0, axis_index_groups=groups)  2.45 us
  transfers between devices with their start and end apart: 5, of which 2 were waited for; matrix products, arithmetic and copies ran while one was open for 0% of the time, Pallas kernels for 3%

profile of v7, /device:TPU:1, one launch (start us, length us, event | category | flops | bytes accessed | tf_op | source)
XLA Modules:
  0.0 84.4 jit_solution(16126492437103709993)
XLA Ops:
  0.6 8.8 %collective-permute-start = (f32[2,128,256]{2,1,0:T(8,128)}, f32[2,128,256]{2,1,0:T(8,128)S(1)}, u32[]{:S(2)}, u32[]{:S(2)}) collective-permute-start(f32[2,128,256]{2,1,0:T(8,128)} %bitcast.3), channel_id=1, source_target_pairs={{0,504},{8,0},{16,8},{24,16},{32,24},{40,32},{48,40},{56,48},{64,5... | collective-permute-start | bytes 786440 | tf_op jit(solution)/shard_map/ppermute | solution.py:303
  9.4 0.0 copy-start.11
  9.4 0.0 copy-start.12
  9.4 0.6 copy-done.11
  10.1 0.0 copy-done.12
  10.1 0.0 copy-start.1
  10.1 0.9 %copy-done.1 = f32[2,1,128,256]{3,2,1,0:T(8,128)S(1)} copy-done((f32[2,1,128,256]{3,2,1,0:T(8,128)S(1)}, f32[2,1,128,256]{3,2,1,0:T(8,128)}, u32[]{:S(2)}) %copy-start.1) | copy-done | bytes 262168
  11.1 0.8 own_windows.1.own
  11.8 0.0 collective-permute-done.rim
  11.8 0.9 %cut_windows.1 = f32[8,2,128,128]{3,2,1,0:T(8,128)S(1)} custom-call(s32[1]{0:T(128)} %bitcast.sec_ref, s32[2]{0:T(128)S(1)} %copy-done.11, s32[2]{0:T(128)S(1)} %copy-done.12, f32[2,2,128,128]{3,2,1,0:T(8,128)S(1)} %own_windows.1.own, f32[2,128,256]{2,1,0:T(8,128)S(1)} %collective-permute-done.rim), custom_call_target="tpu_custom_call" | custom-call | tf_op jit(solution)/shard_map/cut_windows/pallas_call | solution.py:312
  12.8 0.0 copy-start
  12.8 0.0 copy-start.2
  12.8 0.0 copy-start.3
  12.8 0.0 copy-start.4
  12.8 0.0 copy-start.5
  12.8 0.0 copy-start.6
  12.8 0.0 copy-start.7
  12.8 0.0 copy-start.8
  12.9 0.0 copy-start.9
  12.9 0.0 copy-start.10
  12.9 12.7 %all_to_all.20.windows = f32[8,2,128,128]{3,2,1,0:T(8,128)S(1)} all-to-all(f32[8,2,128,128]{3,2,1,0:T(8,128)S(1)} %cut_windows.1), channel_id=1, replica_groups={{7,6,5,4,3,2,1,0},{15,14,13,12,11,10,9,8},{23,22,21,20,19,18,17,16},{31..., dimensions={0} | all-to-all | bytes 2097152 | tf_op jit(solution)/shard_map/all_to_all | solution.py:321
  25.6 0.0 copy-done
  25.6 0.0 copy-done.2
  25.6 0.0 copy-done.3
  25.6 0.0 copy-done.4
  25.6 0.0 copy-done.5
  25.6 0.0 copy-done.6
  25.7 0.0 copy-done.7
  25.7 0.0 copy-done.8
  25.7 0.0 copy-done.9
  25.7 0.0 copy-done.10
  25.7 8.5 %wave_gradients.1 = (f32[2,128,128]{2,1,0:T(8,128)S(1)}, f32[2,128,128]{2,1,0:T(8,128)S(1)}, f32[2,8,16,128]{3,2,1,0:T(8,128)S(1)}) custom-call(s32[1]{0:T(128)} %bitcast.sec_ref, f32[8,2,128,128]{3,2,1,0:T(8,128)S(1)} %all_to_all.20.windows, f32[2,4,128,128]{3,2,1,0:T(8,128)S(1)} %copy-done, f32[2,128,128]{2,1,0:T(8,128)S(1)} %copy-done.2, ...), custom_call_target="tpu_custom_call" | custom-call | tf_op jit(solution)/shard_map/wave_gradients/pallas_call | solution.py:271
  34.2 18.7 %all_to_all.21.blocks = f32[16,16,128]{2,1,0:T(8,128)S(1)} all-to-all(f32[16,16,128]{2,1,0:T(8,128)S(1)} %bitcast.5), channel_id=1, replica_groups={{284,276,268,260,28,20,12,4,280,272,264,256,24,16,8,0},{285,277,269,261..., dimensions={0} | all-to-all | bytes 262144 | tf_op jit(solution)/shard_map/all_to_all | solution.py:260
  52.8 0.6 sum_near.1
  53.5 9.5 %all-to-all-start.2 = ((f32[8,16,128]{2,1,0:T(8,128)}), f32[8,16,128]{2,1,0:T(8,128)S(1)}, u32[]{:S(2)}, u32[]{:S(2)}) async-start(f32[8,16,128]{2,1,0:T(8,128)} %sum_near.1), calls=%async_computation.2 | async-start | bytes 131072 | tf_op jit(solution)/shard_map/all_to_all | solution.py:260
  63.0 2.2 %collective-permute-start.1 = (f32[2,128,128]{2,1,0:T(8,128)S(1)}, f32[2,128,128]{2,1,0:T(8,128)S(1)}, u32[]{:S(2)}, u32[]{:S(2)}) collective-permute-start(f32[2,128,128]{2,1,0:T(8,128)S(1)} %get-tuple-element.9), channel_id=1, source_target_pairs={{0,4},{1,5},{2,6},{3,7},{4,0},{5,1},{6,2},{7,3},{8,12},{9,13},{10,... | collective-permute-start | bytes 393224 | tf_op jit(solution)/shard_map/ppermute | solution.py:327
  65.1 0.1 pad_add_fusion.sec_ref
  65.2 3.8 %collective-permute-done.1.other_grad = f32[2,128,128]{2,1,0:T(8,128)S(1)} collective-permute-done((f32[2,128,128]{2,1,0:T(8,128)S(1)}, f32[2,128,128]{2,1,0:T(8,128)S(1)}, u32[]{:S(2)}, u32[]{:S(2)}) %collective-permute-start.1) | collective-permute-done | bytes 131104 | tf_op jit(solution)/shard_map/ppermute | solution.py:327
  69.0 0.9 %scatter_windows.1 = (f32[2,128,256]{2,1,0:T(8,128)S(1)}, f32[2,128,256]{2,1,0:T(8,128)S(1)}) custom-call(s32[2]{0:T(128)S(1)} %pad_add_fusion.sec_ref, s32[2]{0:T(128)S(1)} %copy-done.11, s32[2]{0:T(128)S(1)} %copy-done.12, f32[2,128,128]{2,1,0:T(8,128)S(1)} %get-tuple-element.8.own_grad, f32[2,128,128]{2,1,0:T(8,128)S(1)} %collective-permute-done.1.other_grad), custom_call_target="tpu_custom_call" | custom-call | tf_op jit(solution)/shard_map/scatter_windows/pallas_call | solution.py:335
  69.9 5.2 %collective-permute-start.2 = (f32[2,128,256]{2,1,0:T(8,128)S(1)}, f32[2,128,256]{2,1,0:T(8,128)S(1)}, u32[]{:S(2)}, u32[]{:S(2)}) collective-permute-start(f32[2,128,256]{2,1,0:T(8,128)S(1)} %get-tuple-element.13), channel_id=1, source_target_pairs={{0,8},{8,16},{16,24},{24,32},{32,40},{40,48},{48,56},{56,64},{64,7... | collective-permute-start | bytes 786440 | tf_op jit(solution)/shard_map/ppermute | solution.py:347
  75.1 0.0 all-to-all-done.2.blocks
  75.1 0.6 sum_far.1
  75.7 5.5 %all-to-all-start.3 = ((f32[8,16,128]{2,1,0:T(8,128)}), f32[8,16,128]{2,1,0:T(8,128)S(1)}, u32[]{:S(2)}, u32[]{:S(2)}) async-start(f32[8,16,128]{2,1,0:T(8,128)} %sum_far.1), calls=%async_computation.3 | async-start | bytes 131072 | tf_op jit(solution)/shard_map/all_to_all | solution.py:260
  81.2 0.0 collective-permute-done.2.received
  81.2 2.4 %all-to-all-done.3.pieces = f32[8,16,128]{2,1,0:T(8,128)S(1)} async-done(((f32[8,16,128]{2,1,0:T(8,128)}), f32[8,16,128]{2,1,0:T(8,128)S(1)}, u32[]{:S(2)}, u32[]{:S(2)}) %all-to-all-start.3) | async-done | bytes 65568 | tf_op jit(solution)/shard_map/all_to_all | solution.py:260
  83.6 0.7 finish.1
Async XLA Ops:
  0.6 11.2 %collective-permute-start = (f32[2,128,256]{2,1,0:T(8,128)}, f32[2,128,256]{2,1,0:T(8,128)S(1)}, u32[]{:S(2)}, u32[]{:S(2)}) collective-permute-start(f32[2,128,256]{2,1,0:T(8,128)} %bitcast.3), channel_id=1, source_target_pairs={{0,504},{8,0},{16,8},{24,16},{32,24},{40,32},{48,40},{56,48},{64,5... | collective-permute-start | bytes 786440 | tf_op jit(solution)/shard_map/ppermute | solution.py:303
  9.4 0.7 copy-start.11
  9.4 0.7 copy-start.12
  10.1 0.9 %copy-start.1 = (f32[2,1,128,256]{3,2,1,0:T(8,128)S(1)}, f32[2,1,128,256]{3,2,1,0:T(8,128)}, u32[]{:S(2)}) copy-start(f32[2,1,128,256]{3,2,1,0:T(8,128)} %param.13) | copy-start | bytes 786436
  12.8 12.9 %copy-start = (f32[2,4,128,128]{3,2,1,0:T(8,128)S(1)}, f32[2,4,128,128]{3,2,1,0:T(8,128)}, u32[]{:S(2)}) copy-start(f32[2,4,128,128]{3,2,1,0:T(8,128)} %probe.1) | copy-start | bytes 1572868
  12.8 12.8 %copy-start.2 = (f32[2,128,128]{2,1,0:T(8,128)S(1)}, f32[2,128,128]{2,1,0:T(8,128)}, u32[]{:S(2)}) copy-start(f32[2,128,128]{2,1,0:T(8,128)} %measured.1) | copy-start | bytes 393220
  12.8 12.8 %copy-start.3 = (bf16[256,256]{1,0:T(8,128)(2,1)S(1)}, bf16[256,256]{1,0:T(8,128)(2,1)}, u32[]{:S(2)}) copy-start(bf16[256,256]{1,0:T(8,128)(2,1)} %constant.22.clone.prop_high) | copy-start | bytes 393220
  12.8 12.8 %copy-start.4 = (bf16[256,256]{1,0:T(8,128)(2,1)S(1)}, bf16[256,256]{1,0:T(8,128)(2,1)}, u32[]{:S(2)}) copy-start(bf16[256,256]{1,0:T(8,128)(2,1)} %constant.23.clone.prop_low) | copy-start | bytes 393220
  12.8 12.8 %copy-start.5 = (bf16[256,256]{1,0:T(8,128)(2,1)S(1)}, bf16[256,256]{1,0:T(8,128)(2,1)}, u32[]{:S(2)}) copy-start(bf16[256,256]{1,0:T(8,128)(2,1)} %constant.24.clone.back_high) | copy-start | bytes 393220
  12.8 12.8 %copy-start.6 = (bf16[256,256]{1,0:T(8,128)(2,1)S(1)}, bf16[256,256]{1,0:T(8,128)(2,1)}, u32[]{:S(2)}) copy-start(bf16[256,256]{1,0:T(8,128)(2,1)} %constant.25.clone.back_low) | copy-start | bytes 393220
  12.8 12.8 %copy-start.7 = (bf16[256,256]{1,0:T(8,128)(2,1)S(1)}, bf16[256,256]{1,0:T(8,128)(2,1)}, u32[]{:S(2)}) copy-start(bf16[256,256]{1,0:T(8,128)(2,1)} %constant.26.clone.four_high) | copy-start | bytes 393220
  12.8 12.8 %copy-start.8 = (bf16[256,256]{1,0:T(8,128)(2,1)S(1)}, bf16[256,256]{1,0:T(8,128)(2,1)}, u32[]{:S(2)}) copy-start(bf16[256,256]{1,0:T(8,128)(2,1)} %constant.27.clone.four_low) | copy-start | bytes 393220
  12.9 12.8 %copy-start.9 = (bf16[256,256]{1,0:T(8,128)(2,1)S(1)}, bf16[256,256]{1,0:T(8,128)(2,1)}, u32[]{:S(2)}) copy-start(bf16[256,256]{1,0:T(8,128)(2,1)} %constant.28.clone.inv_high) | copy-start | bytes 393220
  12.9 12.8 %copy-start.10 = (bf16[256,256]{1,0:T(8,128)(2,1)S(1)}, bf16[256,256]{1,0:T(8,128)(2,1)}, u32[]{:S(2)}) copy-start(bf16[256,256]{1,0:T(8,128)(2,1)} %constant.29.clone.inv_low) | copy-start | bytes 393220
  53.5 21.6 %all-to-all-start.2 = ((f32[8,16,128]{2,1,0:T(8,128)}), f32[8,16,128]{2,1,0:T(8,128)S(1)}, u32[]{:S(2)}, u32[]{:S(2)}) async-start(f32[8,16,128]{2,1,0:T(8,128)} %sum_near.1), calls=%async_computation.2 | async-start | bytes 131072 | tf_op jit(solution)/shard_map/all_to_all | solution.py:260
  63.0 6.0 %collective-permute-start.1 = (f32[2,128,128]{2,1,0:T(8,128)S(1)}, f32[2,128,128]{2,1,0:T(8,128)S(1)}, u32[]{:S(2)}, u32[]{:S(2)}) collective-permute-start(f32[2,128,128]{2,1,0:T(8,128)S(1)} %get-tuple-element.9), channel_id=1, source_target_pairs={{0,4},{1,5},{2,6},{3,7},{4,0},{5,1},{6,2},{7,3},{8,12},{9,13},{10,... | collective-permute-start | bytes 393224 | tf_op jit(solution)/shard_map/ppermute | solution.py:327
  69.9 11.3 %collective-permute-start.2 = (f32[2,128,256]{2,1,0:T(8,128)S(1)}, f32[2,128,256]{2,1,0:T(8,128)S(1)}, u32[]{:S(2)}, u32[]{:S(2)}) collective-permute-start(f32[2,128,256]{2,1,0:T(8,128)S(1)} %get-tuple-element.13), channel_id=1, source_target_pairs={{0,8},{8,16},{16,24},{24,32},{32,40},{40,48},{48,56},{56,64},{64,7... | collective-permute-start | bytes 786440 | tf_op jit(solution)/shard_map/ppermute | solution.py:347
  75.7 7.9 %all-to-all-start.3 = ((f32[8,16,128]{2,1,0:T(8,128)}), f32[8,16,128]{2,1,0:T(8,128)S(1)}, u32[]{:S(2)}, u32[]{:S(2)}) async-start(f32[8,16,128]{2,1,0:T(8,128)} %sum_far.1), calls=%async_computation.3 | async-start | bytes 131072 | tf_op jit(solution)/shard_map/all_to_all | solution.py:260
